TPU v7x, 128 devices: a whole 4x4x4 slice. The times are simulated.
128 devices in a mesh: tile: 16 (over z, y), rep: 8 (over x, core).
Axes of the slice: x: 4, y: 4, z: 4, core: 2. Of those that a mesh axis runs over, the one named last changes fastest.
Arguments:
- patch_features: bfloat16 [8, 4096, 1024], P('rep', 'tile'), may hold values from -6 to 6
- labels: int32 [128, 32], replicated, may hold values from 0 to 3
- assigned_specialists: int32 [8, 4096, 2], P('rep', 'tile'), may hold values from 0 to 15, all different within a row; in each aligned block of 256 rows (0 to 255, 256 to 511, ..., all dimensions but the last counted through in order) at most 48 rows name the same one
- loss_sensitivity: bfloat16 [8, 4096, 1024], P('rep', 'tile'), may hold values from -6 to 6
- attn_qkv: bfloat16 [1024, 3072], replicated, may hold values from -2 to 2, as said below
- attn_out: bfloat16 [1024, 1024], replicated, may hold values from -0.1875 to 0.1875
- router: bfloat16 [1024, 16], replicated, may hold values from -0.1875 to 0.1875
- expert_up: bfloat16 [16, 1024, 2048], P('tile'), may hold values from -0.1875 to 0.1875
- expert_down: bfloat16 [16, 2048, 1024], P('tile'), may hold values from -0.125 to 0.125
Outputs:
- layer_result: bfloat16 [8, 4096, 1024], P('rep', 'tile')
- grad_up: float32 [16, 1024, 2048], P('tile', 'rep')
- grad_down: float32 [16, 2048, 1024], P('tile', None, 'rep')
Inputs may be any that keep to these rules, and one draw needn't show every extreme that they name: `attn_qkv`: Hidden-unit columns of query and key blocks may be strongly aligned in some heads. `assigned_specialists`: within the 256 cells of one strip (aligned blocks of rows), no expert is named by more than 48 cells, a bound that some block reaches of them.
All inputs are finite; a program needn't handle non-finite values.
Results may differ from a plain program's by a relative error of at most 0.018.
Values may be sent and summed in bfloat16 or wider, within the bound.
A program may use at most 128 MiB of HBM per device.

v0:
```python
import functools

import jax
import jax.numpy as jnp
from jax import lax
from jax.experimental import pallas as pl
from jax.experimental.pallas import tpu as pltpu
from jax.sharding import PartitionSpec as P

F = 1024
FFW = 2048
NE = 16
CAP = 48
T = 256
ROWS = NE * CAP
HB = 512
NB = FFW // HB
GROUPS = 2 * NB
QW = 256
SCALE = 32 ** (-0.5)
EPSILON = 1e-05
GELU_A = 0.7978845608028654
GELU_B = 0.044715
f32 = jnp.float32
bf16 = jnp.bfloat16
MESH = pl.DeviceIdType.MESH

NN = (((1,), (0,)), ((), ()))
NT = (((1,), (1,)), ((), ()))
TN = (((0,), (0,)), ((), ()))


def dot(a, b, dims=NN):
    return lax.dot_general(a, b, dims, preferred_element_type=f32)


def iota(shape, dim):
    return lax.broadcasted_iota(jnp.int32, shape, dim)


def layer_norm(values):
    center = values - jnp.mean(values, axis=-1, keepdims=True)
    spread = jnp.mean(center * center, axis=-1, keepdims=True)
    return center * lax.rsqrt(spread + EPSILON)


def norm_to_windows(src, dst, pairs):
    for p in pairs:
        y = layer_norm(src[p * 64 : p * 64 + 64, :].astype(f32))
        y0 = pltpu.roll(y[:32], 28, 0)
        y1 = pltpu.roll(y[32:], 28, 0)
        for w in range(4):
            block = jnp.concatenate([y0[8 * w : 8 * w + 8], y1[8 * w : 8 * w + 8]], axis=0)
            start = (p // 2) * 128 + w * 32 + (p % 2) * 16
            dst[start : start + 16, :] = block.astype(bf16)


def kernel(
    feat, labels, assigned, sens, w_qkv, w_out, router, w_up, w_down,
    out_layer, out_up, out_down,
    feat_v, sens_v, wq, wk, wv, wo, wu, wd,
    halo, n_own, n_halo, q_own, k_all, v_all, ctx, oh, hid, moe,
    disp, disp_t, meta_send, meta_recv, xl_send, xl_recv, ret, a2, hgn, gate_v,
    stage, crecv, r2, rf,
    load_sem, halo_ss, halo_rs, l_ss, l_rs, m_ss, m_rs, x_ss, x_rs, t_ss, t_rs,
    c_ss, c_rs, x2_ss, x2_rs,
):
    me = lax.axis_index("tile")
    rep = lax.axis_index("rep")
    core = lax.rem(rep, 2)
    xpos = lax.div(rep, 2)
    partner = rep + 1 - 2 * core
    x_next = lax.rem(rep + 2, 8)
    x_prev = lax.rem(rep + 6, 8)

    loads = [
        pltpu.make_async_copy(s, d, load_sem.at[i])
        for i, (s, d) in enumerate(
            [
                (feat, feat_v),
                (sens, sens_v),
                (w_qkv.at[:, F : 2 * F], wk),
                (w_qkv.at[:, 2 * F : 3 * F], wv),
                (w_qkv.at[:, 0:F], wq),
                (w_out, wo),
                (w_down, wd),
                (w_up, wu),
            ]
        )
    ]
    for c in loads:
        c.start()
    ld_feat, ld_sens, ld_k, ld_v, ld_q, ld_o, ld_d, ld_u = loads

    barrier = pltpu.get_barrier_semaphore()
    for k in range(1, NE):
        pl.semaphore_signal(barrier, inc=1, device_id={"tile": lax.rem(me + k, NE)}, device_id_type=MESH)
    for r in (partner, x_next, x_prev):
        pl.semaphore_signal(barrier, inc=1, device_id={"rep": r}, device_id_type=MESH)
    pl.semaphore_wait(barrier, NE - 1 + 3)

    def tile_copy(src, dst, ss, rs, target):
        return pltpu.make_async_remote_copy(
            src_ref=src, dst_ref=dst, send_sem=ss, recv_sem=rs,
            device_id={"tile": target}, device_id_type=MESH,
        )

    def rep_copy(src, dst, ss, rs, target):
        return pltpu.make_async_remote_copy(
            src_ref=src, dst_ref=dst, send_sem=ss, recv_sem=rs,
            device_id={"rep": target}, device_id_type=MESH,
        )

    t_next = lax.rem(me + 1, NE)
    t_prev = lax.rem(me + NE - 1, NE)
    halo_copies = [
        tile_copy(feat.at[T // 2 : T, :], halo.at[0 : T // 2, :], halo_ss.at[0], halo_rs.at[0], t_next),
        tile_copy(feat.at[0 : T // 2, :], halo.at[T // 2 : T, :], halo_ss.at[1], halo_rs.at[1], t_prev),
    ]
    for c in halo_copies:
        c.start()

    def exchange(k, src, dst, ss, rs):
        target = lax.rem(me + k, NE)
        return tile_copy(src.at[target], dst.at[me], ss.at[k], rs.at[k], target)

    def arrival(k, src, dst, ss, rs):
        origin = lax.rem(me + NE - k, NE)
        return tile_copy(src.at[origin], dst.at[origin], ss.at[k], rs.at[k], origin)

    a = assigned[...]
    lane = iota((T, 128), 1)
    member = jnp.where((a[:, 0:1] == lane) | (a[:, 1:2] == lane), 1.0, 0.0).astype(bf16)
    eye = (iota((T, T), 0) == iota((T, T), 1)).astype(f32).astype(bf16)
    before = (iota((T, T), 0) < iota((T, T), 1)).astype(f32).astype(bf16)
    member_t = dot(member, eye, TN)[0:NE]
    rank_t = dot(member, before, TN)[0:NE]
    slot_t = jnp.where(member_t > 0.5, rank_t, -1.0)
    slots = iota((CAP, T), 0).astype(f32)
    for e in range(NE):
        disp[e * CAP : (e + 1) * CAP, :] = jnp.where(slot_t[e : e + 1] == slots, 1.0, 0.0).astype(bf16)
    disp[ROWS:, :] = jnp.zeros((128 - CAP, T), bf16)
    id_sum = jnp.sum(member_t * iota((NE, T), 0).astype(f32), axis=0, keepdims=True)
    id_rows = jnp.broadcast_to(id_sum, (16, T)).astype(bf16)

    ld_sens.wait()

    def send_sens(q, _):
        rows = pl.ds(pl.multiple_of(q * 192, 16), 192)
        part = disp[rows, :]
        for n in range(2):
            block = dot(part, sens_v[:, n * 512 : n * 512 + 512]).astype(bf16)
            xl_send[1, pl.ds(q * 4, 4), :, n * 512 : n * 512 + 512] = block.reshape(4, CAP, 512)
        return _

    lax.fori_loop(0, 4, send_sens, 0)

    def make_meta(e, _):
        rows = disp[pl.ds(pl.multiple_of(e * CAP, 16), 128), :]
        meta_send[e] = dot(id_rows, rows, NT).astype(bf16)
        return _

    lax.fori_loop(0, NE, make_meta, 0)
    sens_send, sens_recv = xl_send.at[1], xl_recv.at[1]

    def start_sens(k, _):
        exchange(k, sens_send, sens_recv, l_ss, l_rs).start()
        exchange(k, meta_send, meta_recv, m_ss, m_rs).start()
        return _

    lax.fori_loop(1, NE, start_sens, 0)
    sens_recv[me] = sens_send[me]
    meta_recv[me] = meta_send[me]

    ld_feat.wait()
    norm_to_windows(feat_v, n_own, range(4))

    def project(src, weight, store):
        def body(n, _):
            cols = pl.ds(pl.multiple_of(n * 256, 256), 256)
            store(cols, dot(src[...], weight[:, cols]).astype(bf16))
            return _

        lax.fori_loop(0, 4, body, 0)

    def into(dst, start):
        def store(cols, block):
            dst[:, start : start + 32, cols] = block.reshape(8, 32, 256)

        return store

    def into_q(cols, block):
        q_own[:, cols] = block

    ld_k.wait()
    project(n_own, wk, into(k_all, 0))
    ld_v.wait()
    project(n_own, wv, into(v_all, 0))
    ld_q.wait()
    project(n_own, wq, into_q)

    n = iota((2 * T, 1), 0)
    is_halo = n >= T
    m = jnp.where(is_halo, n - T, n)
    band, win, row4, col8 = m >> 7, (m >> 5) & 3, (m >> 3) & 3, m & 7
    col = (win * 8 + col8 + 4) & 31
    grid_row = me * 8 + jnp.where(is_halo, 12 * band - 4, 4 * band) + row4
    valid = (grid_row >= 0) & (grid_row < 128)
    pick = jnp.where(grid_row == iota((2 * T, 128), 1), 1.0, 0.0).astype(bf16)
    by_row = dot(pick, labels[...].astype(f32).astype(bf16))
    lab = jnp.sum(jnp.where(iota((2 * T, 32), 1) == col, by_row, 0.0), axis=1, keepdims=True)
    lab = jnp.where(valid, lab + jnp.where(col < 4, 4.0, 0.0), -1.0)
    oh[...] = jnp.where(lab == iota((2 * T, 128), 1).astype(f32), 1.0, 0.0).astype(bf16)

    for c in halo_copies:
        c.wait_recv()
    norm_to_windows(halo, n_halo, range(4))
    project(n_halo, wk, into(k_all, 32))
    project(n_halo, wv, into(v_all, 32))

    diag = (iota((QW, QW), 0) >> 5) == (iota((QW, QW), 1) >> 5)

    def window(bw, _):
        rows = pl.ds(pl.multiple_of(bw * 32, 32), 32)
        halo_rows = pl.ds(pl.multiple_of(T + bw * 32, 32), 32)
        oq = oh[rows, :]
        ok = jnp.concatenate([oq, oh[halo_rows, :]], axis=0)
        allowed = dot(ok, jnp.concatenate([oq] * 8, axis=0), NT)
        bias = (allowed - 1.0) * 1e30
        for g in range(4):
            cols = slice(g * QW, (g + 1) * QW)
            qg = jnp.concatenate([q_own[rows, cols]] * 8, axis=0)
            qg = jnp.where(diag, qg, jnp.zeros_like(qg))
            scores = dot(k_all[bw, :, cols], qg, NT) * SCALE + bias
            peak = jnp.max(scores, axis=0, keepdims=True)
            expo = jnp.exp(scores - peak)
            weights = (expo * (1.0 / jnp.sum(expo, axis=0, keepdims=True))).astype(bf16)
            mixed = dot(weights, v_all[bw, :, cols], TN)
            mixed = jnp.where(diag, mixed, 0.0).reshape(8, 32, QW)
            ctx[rows, cols] = jnp.sum(mixed, axis=0).astype(bf16)
        return _

    lax.fori_loop(0, 8, window, 0)

    ld_o.wait()

    def project_out(nn, _):
        cols = pl.ds(pl.multiple_of(nn * 256, 256), 256)
        o = dot(ctx[...], wo[:, cols])
        for r in range(8):
            base = (r // 4) * 128 + (r % 4) * 8
            parts = [o[base + w * 32 : base + w * 32 + 8] for w in range(4)]
            row = pltpu.roll(jnp.concatenate(parts, axis=0), 4, 0)
            hid[r * 32 : r * 32 + 32, cols] = feat_v[r * 32 : r * 32 + 32, cols].astype(f32) + row
        return _

    lax.fori_loop(0, 4, project_out, 0)

    def norm_hidden(r, _):
        rows = pl.ds(pl.multiple_of(r * 64, 64), 64)
        moe[rows, :] = layer_norm(hid[rows, :]).astype(bf16)
        return _

    lax.fori_loop(0, 4, norm_hidden, 0)

    feat_send, feat_recv = xl_send.at[0], xl_recv.at[0]

    def make_feat(q, _):
        rows = pl.ds(pl.multiple_of(q * 192, 16), 192)
        part = disp[rows, :]
        for n in range(2):
            block = dot(part, moe[:, n * 512 : n * 512 + 512]).astype(bf16)
            xl_send[0, pl.ds(q * 4, 4), :, n * 512 : n * 512 + 512] = block.reshape(4, CAP, 512)
        return _

    lax.fori_loop(0, 4, make_feat, 0)

    def start_feat(k, _):
        exchange(k, feat_send, feat_recv, x_ss, x_rs).start()
        return _

    lax.fori_loop(1, NE, start_feat, 0)
    feat_recv[me] = feat_send[me]

    disp_t[...] = disp[0:ROWS, :].T
    ld_u.wait()

    def transpose_up(i, _):
        rows = pl.ds(pl.multiple_of(i * 256, 256), 256)
        wk[rows, :] = wu[:, pl.ds(pl.multiple_of(i * 256, 256), 256)].T
        wv[rows, :] = wu[:, pl.ds(pl.multiple_of(F + i * 256, 256), 256)].T
        return _

    lax.fori_loop(0, 4, transpose_up, 0)
    ld_d.wait()

    def await_sens(k, _):
        arrival(k, sens_send, sens_recv, l_ss, l_rs).wait_recv()
        arrival(k, meta_send, meta_recv, m_ss, m_rs).wait_recv()
        return _

    lax.fori_loop(1, NE, await_sens, 0)

    def first_grads(i, _):
        rows = pl.ds(pl.multiple_of(i * 256, 256), 256)
        block = dot(wd[rows, :], xl_recv[1].reshape(ROWS, F), NT)
        a2[1, pl.ds(pl.multiple_of(i * 256, 256), 256), :] = block.astype(bf16)
        return _

    lax.fori_loop(0, 8, first_grads, 0)

    meta_all = meta_recv[...].reshape(256, 128)
    spread = (iota((128, ROWS), 0) == lax.rem(iota((128, ROWS), 1), CAP)).astype(f32).astype(bf16)
    ids = dot(meta_all, spread)
    own_part = iota((256, ROWS), 0) == lax.div(iota((256, ROWS), 1), CAP) * 16
    other = jnp.sum(jnp.where(own_part, ids, 0.0), axis=0, keepdims=True) - me.astype(f32)
    eye_r = (iota((NE, NE), 0) == iota((NE, NE), 1)).astype(f32).astype(bf16)
    router_t = dot(eye_r, router[...], NT).astype(bf16)

    def await_feat(k, _):
        arrival(k, feat_send, feat_recv, x_ss, x_rs).wait_recv()
        return _

    lax.fori_loop(1, NE, await_feat, 0)

    logits = dot(router_t, xl_recv[0].reshape(ROWS, F), NT)
    sig = 1.0 / (1.0 + jnp.exp(-logits))
    expert = iota((NE, ROWS), 0)
    mine = jnp.sum(jnp.where(expert == me, sig, 0.0), axis=0, keepdims=True)
    others = jnp.sum(jnp.where(expert.astype(f32) == other, sig, 0.0), axis=0, keepdims=True)
    gate_v[...] = jnp.broadcast_to(mine / (mine + others), (8, ROWS))

    def activate(i):
        def run(weight_t, start):
            u = dot(weight_t[pl.ds(pl.multiple_of(start, 256), 256), :], xl_recv[0].reshape(ROWS, F), NT)
            gate = gate_v[0:1, :]
            u2 = u * u
            t = jnp.tanh(GELU_A * u * (1.0 + GELU_B * u2))
            half = 0.5 * (1.0 + t)
            rows = pl.ds(pl.multiple_of(i * 256, 256), 256)
            a2[0, rows, :] = (u * half * gate).astype(bf16)
            slope = half + 0.5 * u * (1.0 - t * t) * (GELU_A + (3.0 * GELU_A * GELU_B) * u2)
            a2[1, rows, :] = (a2[1, rows, :].astype(f32) * gate * slope).astype(bf16)

        @pl.when(i < 4)
        def _():
            run(wk, i * 256)

        @pl.when(i >= 4)
        def _():
            run(wv, (i - 4) * 256)

    def activate_blocks(lo, hi):
        def body(i, _):
            activate(i)
            return _

        lax.fori_loop(lo, hi, body, 0)

    rv_send = sens_send

    def make_results():
        def drain(k, _):
            exchange(k, sens_send, sens_recv, l_ss, l_rs).wait_send()
            return _

        lax.fori_loop(1, NE, drain, 0)
        for half in range(2):
            lanes = slice(half * 384, (half + 1) * 384)

            def turn(i, _):
                cols = pl.ds(pl.multiple_of(i * 256, 256), 256)
                hgn[:, cols] = a2[0, cols, lanes].T
                return _

            lax.fori_loop(0, 8, turn, 0)

            def product(i, _):
                cols = pl.ds(pl.multiple_of(i * 256, 256), 256)
                block = dot(hgn[...], wd[:, cols]).astype(bf16)
                xl_send[1, half * 8 : half * 8 + 8, :, cols] = block.reshape(8, CAP, 256)
                return _

            lax.fori_loop(0, 4, product, 0)

        def start(k, _):
            exchange(k, rv_send, ret, t_ss, t_rs).start()
            return _

        lax.fori_loop(1, NE, start, 0)
        ret[me] = rv_send[me]

    def column_chunk(j):
        shift = jnp.where(j == 0, 2, jnp.where(j == 1, 1, jnp.where(j == 2, 3, 0)))
        return lax.rem(xpos + shift, 4)

    def core_copy(g, j):
        return rep_copy(stage.at[g, j, 1 - core], crecv.at[g, j], c_ss.at[g, j], c_rs.at[g, j], partner)

    def make_pieces(g):
        kind = lax.rem(g, 2)
        hb = lax.div(g, 2)

        def piece(j, _):
            cols = pl.ds(pl.multiple_of(column_chunk(j) * 256, 256), 256)
            for h in range(2):
                rows = pl.ds(pl.multiple_of(hb * HB + h * 256, 256), 256)
                right = xl_recv[1 - kind, :, :, cols].reshape(ROWS, 256)
                block = dot(a2[kind, rows, :], right).astype(bf16)
                stage[g, j, 0, h] = block[:, 0:128]
                stage[g, j, 1, h] = block[:, 128:256]
            core_copy(g, j).start()
            return _

        lax.fori_loop(0, 4, piece, 0)

    def hop(g, which):
        src = [
            stage.at[g, 0, core, 0], stage.at[g, 1, core, 1], stage.at[g, 1, core, 0],
            stage.at[g, 0, core, 1], stage.at[g, 2, core, 0], stage.at[g, 2, core, 1],
        ][which]
        dst = [
            r2.at[g, 0], rf.at[g, 0, 1], rf.at[g, 0, 0],
            r2.at[g, 1], rf.at[g, 1, 0], rf.at[g, 1, 1],
        ][which]
        return rep_copy(src, dst, x2_ss.at[g, which], x2_rs.at[g, which], x_next if which < 3 else x_prev)

    def add_cores(g):
        for j in range(4):
            core_copy(g, j).wait_recv()
            for h in range(2):
                total = stage[g, j, core, h].astype(f32) + crecv[g, j, h].astype(f32)
                stage[g, j, core, h] = total.astype(bf16)
            for which in {0: (0, 3), 1: (1,), 2: (4,), 3: ()}[j]:
                hop(g, which).start()

    def add_far(g):
        hop(g, 0).wait_recv()
        total = stage[g, 1, core, 0].astype(f32) + r2[g, 0].astype(f32)
        stage[g, 1, core, 0] = total.astype(bf16)
        hop(g, 2).start()
        hop(g, 3).wait_recv()
        total = stage[g, 2, core, 1].astype(f32) + r2[g, 1].astype(f32)
        stage[g, 2, core, 1] = total.astype(bf16)
        hop(g, 5).start()

    def finish(g):
        for which in (1, 2, 4, 5):
            hop(g, which).wait_recv()
        hb = lax.div(g, 2)
        for h in range(2):
            total = (
                stage[g, 3, core, h].astype(f32)
                + rf[g, 0, h].astype(f32)
                + rf[g, 1, h].astype(f32)
            )
            start = pl.multiple_of(hb * HB + h * 256, 256)

            @pl.when(lax.rem(g, 2) == 0)
            def _():
                out_down[pl.ds(start, 256), :] = total

            @pl.when(lax.rem(g, 2) == 1)
            def _():
                out_up[:, pl.ds(start, 256)] = total.T

    def step(s, carry):
        @pl.when(s == 0)
        def _():
            activate_blocks(0, 2)

        @pl.when(s == 1)
        def _():
            activate_blocks(2, 6)

        @pl.when(s == 2)
        def _():
            activate_blocks(6, 8)

        @pl.when(s < GROUPS)
        def _():
            make_pieces(s)

        @pl.when((s >= 1) & (s < GROUPS + 1))
        def _():
            add_cores(s - 1)

        @pl.when((s >= 2) & (s < GROUPS + 2))
        def _():
            add_far(s - 2)

        @pl.when(s >= 3)
        def _():
            finish(s - 3)

        @pl.when(s == 2)
        def _():
            make_results()

        return carry

    lax.fori_loop(0, GROUPS + 3, step, 0)

    def await_results(k, _):
        arrival(k, rv_send, ret, t_ss, t_rs).wait_recv()
        return _

    lax.fori_loop(1, NE, await_results, 0)

    def combine(i, _):
        cols = pl.ds(pl.multiple_of(i * 256, 256), 256)
        mixture = dot(disp_t[...], ret[:, :, cols].reshape(ROWS, 256))
        out_layer[:, cols] = (hid[:, cols] + mixture).astype(bf16)
        return _

    lax.fori_loop(0, 4, combine, 0)

    for c in halo_copies:
        c.wait_send()

    def drain_tiles(k, _):
        exchange(k, meta_send, meta_recv, m_ss, m_rs).wait_send()
        exchange(k, feat_send, feat_recv, x_ss, x_rs).wait_send()
        exchange(k, rv_send, ret, t_ss, t_rs).wait_send()
        return _

    lax.fori_loop(1, NE, drain_tiles, 0)

    def drain_groups(g, _):
        for j in range(4):
            core_copy(g, j).wait_send()
        for which in range(6):
            hop(g, which).wait_send()
        return _

    lax.fori_loop(0, GROUPS, drain_groups, 0)


def on_device(
    patch_features, labels, assigned_specialists, loss_sensitivity,
    attn_qkv, attn_out, router, expert_up, expert_down,
):
    hbm = pl.BlockSpec(memory_space=pl.ANY)
    vmem = pl.BlockSpec(memory_space=pltpu.VMEM)
    dma = pltpu.SemaphoreType.DMA

    def buf(*shape, dtype=bf16):
        return pltpu.VMEM(shape, dtype)

    scratch = [
        buf(T, F), buf(T, F), buf(F, F), buf(F, F), buf(F, F), buf(F, F), buf(F, FFW), buf(FFW, F),
        buf(T, F), buf(T, F), buf(T, F), buf(T, F), buf(8, 64, F), buf(8, 64, F), buf(T, F),
        buf(2 * T, 128), buf(T, F, dtype=f32), buf(T, F),
        buf(ROWS + 128 - CAP, T), buf(T, ROWS), buf(NE, 16, 128), buf(NE, 16, 128),
        buf(2, NE, CAP, F), buf(2, NE, CAP, F), buf(NE, CAP, F), buf(2, FFW, ROWS),
        buf(ROWS // 2, FFW), buf(8, ROWS, dtype=f32),
        buf(GROUPS, 4, 2, 2, 256, 128), buf(GROUPS, 4, 2, 256, 128),
        buf(GROUPS, 2, 256, 128), buf(GROUPS, 2, 2, 256, 128),
        dma((8,)), dma((2,)), dma((2,)),
        dma((NE,)), dma((NE,)), dma((NE,)), dma((NE,)), dma((NE,)), dma((NE,)), dma((NE,)), dma((NE,)),
        dma((GROUPS, 4)), dma((GROUPS, 4)), dma((GROUPS, 6)), dma((GROUPS, 6)),
    ]
    layer, up, down = pl.pallas_call(
        kernel,
        out_shape=(
            jax.ShapeDtypeStruct((T, F), bf16),
            jax.ShapeDtypeStruct((F // 8, FFW), f32),
            jax.ShapeDtypeStruct((FFW, F // 8), f32),
        ),
        in_specs=[hbm, vmem, vmem, hbm, hbm, hbm, vmem, hbm, hbm],
        out_specs=(vmem, vmem, vmem),
        scratch_shapes=scratch,
        compiler_params=pltpu.CompilerParams(
            collective_id=0, has_side_effects=True, vmem_limit_bytes=62 * 1024 * 1024
        ),
        name="layer",
    )(
        patch_features[0], labels, assigned_specialists[0], loss_sensitivity[0],
        attn_qkv, attn_out, router, expert_up[0], expert_down[0],
    )
    return layer[None], up[None], down[None]


def solution(mesh):
    return jax.shard_map(
        on_device,
        mesh=mesh,
        in_specs=(
            P("rep", "tile", None), P(), P("rep", "tile", None), P("rep", "tile", None),
            P(), P(), P(), P("tile", None, None), P("tile", None, None),
        ),
        out_specs=(P("rep", "tile", None), P("tile", "rep", None), P("tile", None, "rep")),
        check_vma=False,
    )
```

profile of v0, /device:TPU:2, one launch (start us, length us, event | category | flops | bytes accessed | tf_op | source)
XLA Modules:
  0.0 124.5 jit_solution(14439695031152391283)
XLA Ops:
  0.6 1.4 %copy.13.labels = s32[128,32]{1,0:T(8,128)} copy(s32[128,32]{0,1:T(8,128)} %param.10) | data formatting | bytes 32768 | tf_op args[1]
  2.1 1.5 %copy.12 = s32[1,256,2]{2,1,0:T(8,128)} copy(s32[1,256,2]{1,2,0:T(2,128)} %param.11) | data formatting | bytes 4096 | tf_op args[2]
  3.6 1.6 %copy.14.router = bf16[1024,16]{1,0:T(8,128)(2,1)} copy(bf16[1024,16]{0,1:T(8,128)(2,1)} %param.15) | data formatting | bytes 65536 | tf_op args[6]
  5.2 113.0 %layer.1 = (bf16[256,1024]{1,0:T(8,128)(2,1)}, f32[128,2048]{1,0:T(8,128)}, f32[2048,128]{1,0:T(8,128)}) custom-call(bf16[256,1024]{1,0:T(8,128)(2,1)} %bitcast.13, s32[128,32]{1,0:T(8,128)} %copy.13.labels, s32[256,2]{1,0:T(8,128)} %bitcast.12, bf16[256,1024]{1,0:T(8,128)(2,1)} %bitcast.14, bf16[1024,3072]{1,0:T(8,128)(2,1)} %w_qkv.1, ...), custom_call_target="tpu_custom_call" | custom-call | tf_op jit(solution)/shard_map/layer/pallas_call | solution.py:563
  118.1 1.9 %copy.18 = bf16[1,256,1024]{2,1,0:T(8,128)(2,1)} copy(bf16[1,256,1024]{2,1,0:T(8,128)(2,1)} %bitcast.15) | data formatting | bytes 1048576
  120.0 2.3 %copy.19 = f32[1,128,2048]{2,1,0:T(8,128)} copy(f32[1,128,2048]{2,1,0:T(8,128)} %bitcast.11) | data formatting | bytes 2097152
  122.3 2.3 %copy.20 = f32[1,2048,128]{2,1,0:T(8,128)} copy(f32[1,2048,128]{2,1,0:T(8,128)} %bitcast.10) | data formatting | bytes 2097152
where the time goes:
time: 125 us
  Pallas kernels  113 us (90%)
  local copies, waits for them, and re-layouts  10.9 us (9%)
    pallas_call x1, Pallas kernels, on_device(): pl.pallas_call(kernel, out_shape=(jax.ShapeDtypeStruct((T, F), bf16), jax...  113 us
    unnamed x6, local copies, waits for them, and re-layouts  10.9 us

commit v1 on v0

v1 whole, which is shorter than its diff:
```python
import functools

import jax
import jax.numpy as jnp
from jax import lax
from jax.experimental import pallas as pl
from jax.experimental.pallas import tpu as pltpu
from jax.sharding import PartitionSpec as P

F = 1024
FFW = 2048
NE = 16
CAP = 48
T = 256
ROWS = NE * CAP
HB = 512
NB = FFW // HB
GROUPS = 2 * NB
EARLY = 6
OFFSETS = sorted(
    [(a, b) for a in range(4) for b in range(4) if (a, b) != (0, 0)],
    key=lambda o: -(min(o[0], 4 - o[0]) + min(o[1], 4 - o[1])),
)
QW = 256
SCALE = 32 ** (-0.5)
EPSILON = 1e-05
GELU_A = 0.7978845608028654
GELU_B = 0.044715
f32 = jnp.float32
bf16 = jnp.bfloat16
MESH = pl.DeviceIdType.MESH

NN = (((1,), (0,)), ((), ()))
NT = (((1,), (1,)), ((), ()))
TN = (((0,), (0,)), ((), ()))


def dot(a, b, dims=NN):
    return lax.dot_general(a, b, dims, preferred_element_type=f32)


def iota(shape, dim):
    return lax.broadcasted_iota(jnp.int32, shape, dim)


def layer_norm(values):
    center = values - jnp.mean(values, axis=-1, keepdims=True)
    spread = jnp.mean(center * center, axis=-1, keepdims=True)
    return center * lax.rsqrt(spread + EPSILON)


def norm_to_windows(src, dst, pairs):
    for p in pairs:
        y = layer_norm(src[p * 64 : p * 64 + 64, :].astype(f32))
        y0 = pltpu.roll(y[:32], 28, 0)
        y1 = pltpu.roll(y[32:], 28, 0)
        for w in range(4):
            block = jnp.concatenate([y0[8 * w : 8 * w + 8], y1[8 * w : 8 * w + 8]], axis=0)
            start = (p // 2) * 128 + w * 32 + (p % 2) * 16
            dst[start : start + 16, :] = block.astype(bf16)


def kernel(
    feat, labels, assigned, sens, w_qkv, w_out, router, w_up, w_down,
    out_layer, out_up, out_down,
    feat_v, sens_v, wq, wk, wv, wo, wu, wd,
    halo, n_own, n_halo, q_own, k_all, v_all, ctx, oh, hid, moe,
    disp, disp_t, meta_send, meta_recv, xl_send, xl_recv, ret, a2, gate_v,
    stage, crecv, r2, rf,
    load_sem, halo_ss, halo_rs, l_ss, l_rs, m_ss, m_rs, x_ss, x_rs, t_ss, t_rs,
    c_ss, c_rs, x2_ss, x2_rs,
):
    me = lax.axis_index("tile")
    rep = lax.axis_index("rep")
    core = lax.rem(rep, 2)
    xpos = lax.div(rep, 2)
    partner = rep + 1 - 2 * core
    x_next = lax.rem(rep + 2, 8)
    x_prev = lax.rem(rep + 6, 8)

    loads = [
        pltpu.make_async_copy(s, d, load_sem.at[i])
        for i, (s, d) in enumerate(
            [
                (feat, feat_v),
                (sens, sens_v),
                (w_qkv.at[:, F : 2 * F], wk),
                (w_qkv.at[:, 2 * F : 3 * F], wv),
                (w_qkv.at[:, 0:F], wq),
                (w_out, wo),
                (w_down, wd),
                (w_up, wu),
            ]
        )
    ]
    for c in loads[:5]:
        c.start()
    ld_feat, ld_sens, ld_k, ld_v, ld_q, ld_o, ld_d, ld_u = loads

    barrier = pltpu.get_barrier_semaphore()
    y, z = lax.rem(me, 4), lax.div(me, 4)
    to_tile = [lax.rem(z + b, 4) * 4 + lax.rem(y + a, 4) for a, b in OFFSETS]
    from_tile = [lax.rem(z + 4 - b, 4) * 4 + lax.rem(y + 4 - a, 4) for a, b in OFFSETS]
    for t in to_tile:
        pl.semaphore_signal(barrier, inc=1, device_id={"tile": t}, device_id_type=MESH)
    for r in (partner, x_next, x_prev):
        pl.semaphore_signal(barrier, inc=1, device_id={"rep": r}, device_id_type=MESH)
    pl.semaphore_wait(barrier, NE - 1 + 3)

    def tile_copy(src, dst, ss, rs, target):
        return pltpu.make_async_remote_copy(
            src_ref=src, dst_ref=dst, send_sem=ss, recv_sem=rs,
            device_id={"tile": target}, device_id_type=MESH,
        )

    def rep_copy(src, dst, ss, rs, target):
        return pltpu.make_async_remote_copy(
            src_ref=src, dst_ref=dst, send_sem=ss, recv_sem=rs,
            device_id={"rep": target}, device_id_type=MESH,
        )

    t_next = lax.rem(me + 1, NE)
    t_prev = lax.rem(me + NE - 1, NE)
    halo_copies = [
        tile_copy(feat.at[T // 2 : T, :], halo.at[0 : T // 2, :], halo_ss.at[0], halo_rs.at[0], t_next),
        tile_copy(feat.at[0 : T // 2, :], halo.at[T // 2 : T, :], halo_ss.at[1], halo_rs.at[1], t_prev),
    ]
    for c in halo_copies:
        c.start()

    def exchange(i, src, dst, ss, rs):
        t = to_tile[i]
        return tile_copy(src.at[t], dst.at[me], ss.at[i], rs.at[i], t)

    def arrival(i, src, dst, ss, rs):
        t = from_tile[i]
        return tile_copy(src.at[t], dst.at[t], ss.at[i], rs.at[i], t)

    others = range(NE - 1)

    ids_t = assigned[...]
    expert = iota((NE, T), 0)
    member_t = jnp.where((ids_t[0:1] == expert) | (ids_t[1:2] == expert), 1.0, 0.0)
    before = (iota((T, T), 0) < iota((T, T), 1)).astype(f32).astype(bf16)
    rank_t = dot(member_t.astype(bf16), before)
    slot_t = jnp.where(member_t > 0.5, rank_t, -1.0)
    slots = iota((CAP, T), 0).astype(f32)
    for e in range(NE):
        disp[e * CAP : (e + 1) * CAP, :] = jnp.where(slot_t[e : e + 1] == slots, 1.0, 0.0).astype(bf16)
    disp[ROWS:, :] = jnp.zeros((128 - CAP, T), bf16)
    id_sum = jnp.sum(member_t * expert.astype(f32), axis=0, keepdims=True)
    id_rows = jnp.broadcast_to(id_sum, (16, T)).astype(bf16)

    ld_sens.wait()

    def dispatch(src, kind):
        for n in range(2):
            cols = slice(n * 512, n * 512 + 512)
            block = dot(disp[0:ROWS, :], src[:, cols]).astype(bf16)
            xl_send[kind, :, :, cols] = block.reshape(NE, CAP, 512)

    dispatch(sens_v, 1)

    def make_meta(e, _):
        rows = disp[pl.ds(pl.multiple_of(e * CAP, 16), 128), :]
        meta_send[e] = dot(id_rows, rows, NT).astype(bf16)
        return _

    lax.fori_loop(0, NE, make_meta, 0)
    sens_send, sens_recv = xl_send.at[1], xl_recv.at[1]

    def start_sens(which):
        for i in which:
            exchange(i, sens_send, sens_recv, l_ss, l_rs).start()
            exchange(i, meta_send, meta_recv, m_ss, m_rs).start()

    start_sens(range(EARLY))
    sens_recv[me] = sens_send[me]
    meta_recv[me] = meta_send[me]

    ld_feat.wait()
    norm_to_windows(feat_v, n_own, range(4))

    def project(src, weight, dst, start):
        block = dot(src[...], weight[...]).astype(bf16)
        dst[:, start : start + 32, :] = block.reshape(8, 32, F)

    ld_k.wait()
    project(n_own, wk, k_all, 0)
    ld_v.wait()
    project(n_own, wv, v_all, 0)
    ld_q.wait()
    q_own[...] = dot(n_own[...], wq[...]).astype(bf16)
    for c in loads[5:]:
        c.start()

    n = iota((2 * T, 1), 0)
    is_halo = n >= T
    m = jnp.where(is_halo, n - T, n)
    band, win, row4, col8 = m >> 7, (m >> 5) & 3, (m >> 3) & 3, m & 7
    col = (win * 8 + col8 + 4) & 31
    grid_row = me * 8 + jnp.where(is_halo, 12 * band - 4, 4 * band) + row4
    valid = (grid_row >= 0) & (grid_row < 128)
    pick = jnp.where(grid_row == iota((2 * T, 128), 1), 1.0, 0.0).astype(bf16)
    by_row = dot(pick, labels[...].astype(f32).astype(bf16), NT)
    lab = jnp.sum(jnp.where(iota((2 * T, 32), 1) == col, by_row, 0.0), axis=1, keepdims=True)
    lab = jnp.where(valid, lab + jnp.where(col < 4, 4.0, 0.0), -1.0)
    oh[...] = jnp.where(lab == iota((2 * T, 128), 1).astype(f32), 1.0, 0.0).astype(bf16)

    for c in halo_copies:
        c.wait_recv()
    norm_to_windows(halo, n_halo, range(4))
    project(n_halo, wk, k_all, 32)
    project(n_halo, wv, v_all, 32)

    diag = (iota((QW, QW), 0) >> 5) == (iota((QW, QW), 1) >> 5)

    def window_row(b, _):
        parts = []
        for w in range(4):
            bw = b * 4 + w
            rows = pl.ds(pl.multiple_of(bw * 32, 32), 32)
            halo_rows = pl.ds(pl.multiple_of(T + bw * 32, 32), 32)
            oq = oh[rows, :]
            ok = jnp.concatenate([oq, oh[halo_rows, :]], axis=0)
            bias = jnp.concatenate([(dot(oq, ok, NT) - 1.0) * 1e30] * 8, axis=0)
            parts += [(bw, rows, slice(g * QW, (g + 1) * QW), bias) for g in range(4)]
        all_scores = []
        for bw, rows, cols, bias in parts:
            qg = jnp.concatenate([q_own[rows, cols]] * 8, axis=0)
            qg = jnp.where(diag, qg, jnp.zeros_like(qg))
            all_scores.append(dot(qg, k_all[bw, :, cols], NT) * SCALE + bias)
        all_weights = []
        for scores in all_scores:
            expo = jnp.exp(scores - jnp.max(scores, axis=1, keepdims=True))
            all_weights.append((expo * (1.0 / jnp.sum(expo, axis=1, keepdims=True))).astype(bf16))
        for (bw, rows, cols, bias), weights in zip(parts, all_weights):
            mixed = dot(weights, v_all[bw, :, cols])
            mixed = jnp.where(diag, mixed, 0.0).reshape(8, 32, QW)
            ctx[rows, cols] = jnp.sum(mixed, axis=0).astype(bf16)
        return _

    lax.fori_loop(0, 2, window_row, 0)

    ld_o.wait()

    o = dot(ctx[...], wo[...])
    for r in range(8):
        base = (r // 4) * 128 + (r % 4) * 8
        parts = [o[base + w * 32 : base + w * 32 + 8] for w in range(4)]
        row = pltpu.roll(jnp.concatenate(parts, axis=0), 4, 0)
        hid[r * 32 : r * 32 + 32, :] = feat_v[r * 32 : r * 32 + 32, :].astype(f32) + row

    def norm_hidden(r, _):
        rows = pl.ds(pl.multiple_of(r * 64, 64), 64)
        moe[rows, :] = layer_norm(hid[rows, :]).astype(bf16)
        return _

    lax.fori_loop(0, 4, norm_hidden, 0)

    feat_send, feat_recv = xl_send.at[0], xl_recv.at[0]

    dispatch(moe, 0)
    for i in others:
        exchange(i, feat_send, feat_recv, x_ss, x_rs).start()
    start_sens(range(EARLY, NE - 1))
    feat_recv[me] = feat_send[me]

    disp_t[...] = disp[0:ROWS, :].T
    ld_u.wait()

    def transpose_up(i, _):
        rows = pl.ds(pl.multiple_of(i * 256, 256), 256)
        wk[rows, :] = wu[:, pl.ds(pl.multiple_of(i * 256, 256), 256)].T
        wv[rows, :] = wu[:, pl.ds(pl.multiple_of(F + i * 256, 256), 256)].T
        return _

    lax.fori_loop(0, 4, transpose_up, 0)

    for i in others:
        arrival(i, meta_send, meta_recv, m_ss, m_rs).wait_recv()

    meta_all = meta_recv[...].reshape(256, 128)
    spread = (iota((128, ROWS), 0) == lax.rem(iota((128, ROWS), 1), CAP)).astype(f32).astype(bf16)
    ids = dot(meta_all, spread)
    own_part = iota((256, ROWS), 0) == lax.div(iota((256, ROWS), 1), CAP) * 16
    other = jnp.sum(jnp.where(own_part, ids, 0.0), axis=0, keepdims=True) - me.astype(f32)

    for i in others:
        arrival(i, feat_send, feat_recv, x_ss, x_rs).wait_recv()

    logits = dot(router[...], xl_recv[0].reshape(ROWS, F), NT)
    sig = 1.0 / (1.0 + jnp.exp(-logits))
    expert = iota((NE, ROWS), 0)
    mine = jnp.sum(jnp.where(expert == me, sig, 0.0), axis=0, keepdims=True)
    theirs = jnp.sum(jnp.where(expert.astype(f32) == other, sig, 0.0), axis=0, keepdims=True)
    gate_v[...] = jnp.broadcast_to(mine / (mine + theirs), (8, ROWS))

    def activate(weight_t, half):
        def body(i, _):
            start = pl.multiple_of(i * HB, HB)
            u = dot(weight_t[pl.ds(start, HB), :], xl_recv[0].reshape(ROWS, F), NT)
            gate = gate_v[0:1, :]
            u2 = u * u
            t = jnp.tanh(GELU_A * u * (1.0 + GELU_B * u2))
            rise = 0.5 * (1.0 + t)
            rows = pl.ds(pl.multiple_of(half * F + i * HB, HB), HB)
            a2[0, rows, :] = (u * rise * gate).astype(bf16)
            slope = rise + 0.5 * u * (1.0 - t * t) * (GELU_A + (3.0 * GELU_A * GELU_B) * u2)
            a2[1, rows, :] = (slope * gate).astype(bf16)
            return _

        lax.fori_loop(0, F // HB, body, 0)

    activate(wk, 0)
    activate(wv, 1)
    ld_d.wait()
    for i in others:
        arrival(i, sens_send, sens_recv, l_ss, l_rs).wait_recv()

    def first_grads():
        def body(i, _):
            rows = pl.ds(pl.multiple_of(i * HB, HB), HB)
            block = dot(wd[rows, :], xl_recv[1].reshape(ROWS, F), NT)
            a2[1, rows, :] = (block * a2[1, rows, :].astype(f32)).astype(bf16)
            return _

        lax.fori_loop(0, NB, body, 0)

    rv_send = sens_send

    def drain_sens():
        for i in others:
            exchange(i, sens_send, sens_recv, l_ss, l_rs).wait_send()

    def make_results(half):
        lanes = slice(half * 384, (half + 1) * 384)

        def product(i, _):
            cols = pl.ds(pl.multiple_of(i * 512, 512), 512)
            block = dot(a2[0, :, lanes], wd[:, cols], TN).astype(bf16)
            xl_send[1, half * 8 : half * 8 + 8, :, cols] = block.reshape(8, CAP, 512)
            return _

        lax.fori_loop(0, 2, product, 0)

    def send_results():
        for i in others:
            exchange(i, rv_send, ret, t_ss, t_rs).start()
        ret[me] = rv_send[me]

    def chunk(away):
        return lax.rem(xpos + away, 4)

    def core_copy(g):
        return rep_copy(stage.at[g, 1 - core], crecv.at[g], c_ss.at[g], c_rs.at[g], partner)

    def make_pieces(g):
        kind = lax.div(g, NB)
        rows = pl.ds(pl.multiple_of(lax.rem(g, NB) * HB, HB), HB)
        block = dot(a2[kind, rows, :], xl_recv[1 - kind].reshape(ROWS, F)).astype(bf16)
        for q in range(4):
            for c in range(2):
                for h in range(2):
                    start = (2 * q + c) * 128
                    stage[g, c, q, h] = block[h * 256 : h * 256 + 256, start : start + 128]
        core_copy(g).start()

    def hop(g, which):
        away, h = [(2, 0), (1, 1), (1, 0), (2, 1), (3, 0), (3, 1)][which]
        dst = [
            r2.at[g, 0], rf.at[g, 0, 1], rf.at[g, 0, 0],
            r2.at[g, 1], rf.at[g, 1, 0], rf.at[g, 1, 1],
        ][which]
        src = stage.at[g, core, chunk(away), h]
        return rep_copy(src, dst, x2_ss.at[g, which], x2_rs.at[g, which], x_next if which < 3 else x_prev)

    def add_cores(g):
        core_copy(g).wait_recv()
        for away, sends in ((2, (0, 3)), (1, (1,)), (3, (4,)), (0, ())):
            q = chunk(away)
            for h in range(2):
                total = stage[g, core, q, h].astype(f32) + crecv[g, q, h].astype(f32)
                stage[g, core, q, h] = total.astype(bf16)
            for which in sends:
                hop(g, which).start()

    def add_far(g):
        for first, away, h, second in ((0, 1, 0, 2), (3, 3, 1, 5)):
            hop(g, first).wait_recv()
            q = chunk(away)
            total = stage[g, core, q, h].astype(f32) + r2[g, h].astype(f32)
            stage[g, core, q, h] = total.astype(bf16)
            hop(g, second).start()

    def finish(g):
        for which in (1, 2, 4, 5):
            hop(g, which).wait_recv()
        hb = lax.rem(g, NB)
        for h in range(2):
            total = (
                stage[g, core, xpos, h].astype(f32)
                + rf[g, 0, h].astype(f32)
                + rf[g, 1, h].astype(f32)
            )
            start = pl.multiple_of(hb * HB + h * 256, 256)

            @pl.when(g < NB)
            def _():
                out_down[pl.ds(start, 256), :] = total

            @pl.when(g >= NB)
            def _():
                out_up[:, pl.ds(start, 256)] = total.T

    def step(s, carry):
        @pl.when(s < GROUPS)
        def _():
            make_pieces(s)

        @pl.when((s >= 1) & (s < GROUPS + 1))
        def _():
            add_cores(s - 1)

        @pl.when((s >= 2) & (s < GROUPS + 2))
        def _():
            add_far(s - 2)

        @pl.when(s >= 3)
        def _():
            finish(s - 3)

        @pl.when(s == 2)
        def _():
            drain_sens()
            make_results(0)

        @pl.when(s == 3)
        def _():
            first_grads()

        @pl.when(s == 4)
        def _():
            make_results(1)
            send_results()

        return carry

    lax.fori_loop(0, GROUPS + 3, step, 0)

    for i in others:
        arrival(i, rv_send, ret, t_ss, t_rs).wait_recv()

    def combine(i, _):
        cols = pl.ds(pl.multiple_of(i * 256, 256), 256)
        mixture = dot(disp_t[...], ret[:, :, cols].reshape(ROWS, 256))
        out_layer[:, cols] = (hid[:, cols] + mixture).astype(bf16)
        return _

    lax.fori_loop(0, 4, combine, 0)

    for c in halo_copies:
        c.wait_send()

    for i in others:
        exchange(i, meta_send, meta_recv, m_ss, m_rs).wait_send()
        exchange(i, feat_send, feat_recv, x_ss, x_rs).wait_send()
        exchange(i, rv_send, ret, t_ss, t_rs).wait_send()

    def drain_groups(g, _):
        core_copy(g).wait_send()
        for which in range(6):
            hop(g, which).wait_send()
        return _

    lax.fori_loop(0, GROUPS, drain_groups, 0)


def hand_over(layer, up, down, out_layer, out_up, out_down):
    out_layer[...] = layer[...]
    out_up[...] = up[...]
    out_down[...] = down[...]


def on_device(
    patch_features, labels, assigned_specialists, loss_sensitivity,
    attn_qkv, attn_out, router, expert_up, expert_down,
):
    hbm = pl.BlockSpec(memory_space=pl.ANY)
    vmem = pl.BlockSpec(memory_space=pltpu.VMEM)
    dma = pltpu.SemaphoreType.DMA

    def buf(*shape, dtype=bf16):
        return pltpu.VMEM(shape, dtype)

    scratch = [
        buf(T, F), buf(T, F), buf(F, F), buf(F, F), buf(F, F), buf(F, F), buf(F, FFW), buf(FFW, F),
        buf(T, F), buf(T, F), buf(T, F), buf(T, F), buf(8, 64, F), buf(8, 64, F), buf(T, F),
        buf(2 * T, 128), buf(T, F, dtype=f32), buf(T, F),
        buf(ROWS + 128 - CAP, T), buf(T, ROWS), buf(NE, 16, 128), buf(NE, 16, 128),
        buf(2, NE, CAP, F), buf(2, NE, CAP, F), buf(NE, CAP, F), buf(2, FFW, ROWS),
        buf(8, ROWS, dtype=f32),
        buf(GROUPS, 2, 4, 2, 256, 128), buf(GROUPS, 4, 2, 256, 128),
        buf(GROUPS, 2, 256, 128), buf(GROUPS, 2, 2, 256, 128),
        dma((8,)), dma((2,)), dma((2,)),
        dma((NE,)), dma((NE,)), dma((NE,)), dma((NE,)), dma((NE,)), dma((NE,)), dma((NE,)), dma((NE,)),
        dma((GROUPS,)), dma((GROUPS,)), dma((GROUPS, 6)), dma((GROUPS, 6)),
    ]
    layer, up, down = pl.pallas_call(
        kernel,
        out_shape=(
            jax.ShapeDtypeStruct((T, F), bf16),
            jax.ShapeDtypeStruct((F // 8, FFW), f32),
            jax.ShapeDtypeStruct((FFW, F // 8), f32),
        ),
        in_specs=[hbm, vmem, vmem, hbm, hbm, hbm, vmem, hbm, hbm],
        out_specs=(vmem, vmem, vmem),
        scratch_shapes=scratch,
        compiler_params=pltpu.CompilerParams(
            collective_id=0, has_side_effects=True, vmem_limit_bytes=62 * 1024 * 1024
        ),
        name="layer",
    )(
        patch_features[0], labels.T, assigned_specialists[0].T, loss_sensitivity[0],
        attn_qkv, attn_out, router.T, expert_up[0], expert_down[0],
    )
    blocks = [pl.BlockSpec(shape, lambda i: (i, 0)) for shape in ((64, F), (32, FFW), (512, 128))]
    layer, up, down = pl.pallas_call(
        hand_over,
        out_shape=(
            jax.ShapeDtypeStruct((T, F), bf16),
            jax.ShapeDtypeStruct((F // 8, FFW), f32),
            jax.ShapeDtypeStruct((FFW, F // 8), f32),
        ),
        grid=(4,),
        in_specs=blocks,
        out_specs=tuple(blocks),
        name="hand_over",
    )(layer, up, down)
    return layer[None], up[None], down[None]


def solution(mesh):
    return jax.shard_map(
        on_device,
        mesh=mesh,
        in_specs=(
            P("rep", "tile", None), P(), P("rep", "tile", None), P("rep", "tile", None),
            P(), P(), P(), P("tile", None, None), P("tile", None, None),
        ),
        out_specs=(P("rep", "tile", None), P("tile", "rep", None), P("tile", None, "rep")),
        check_vma=False,
    )
```

time: 125 us -> 114 us (0.912)
  the two profiles are of different devices: /device:TPU:2 before, /device:TPU:1 now
where the time goes in v1:
time: 114 us; the launch traced here: 113 us
  Pallas kernels  112 us (98%)
    pallas_call x1, Pallas kernels, on_device(): pl.pallas_call(kernel, out_shape=(jax.ShapeDtypeStruct((T, F), bf16), jax...  108 us
    pallas_call x1, Pallas kernels, on_device(): pl.pallas_call(hand_over, out_shape=(jax.ShapeDtypeStruct((T, F), bf16),...  3.97 us

profile of v1, /device:TPU:1, one launch (start us, length us, event | category | flops | bytes accessed | tf_op | source)
XLA Modules:
  0.0 112.7 jit_solution(922447661821189856)
XLA Ops:
  0.6 108.1 %layer.1 = (bf16[256,1024]{1,0:T(8,128)(2,1)}, f32[128,2048]{1,0:T(8,128)}, f32[2048,128]{1,0:T(8,128)}) custom-call(bf16[256,1024]{1,0:T(8,128)(2,1)} %bitcast.14, s32[32,128]{1,0:T(8,128)} %bitcast.17, s32[2,256]{1,0:T(2,128)} %bitcast.18, bf16[256,1024]{1,0:T(8,128)(2,1)} %bitcast.15, bf16[1024,3072]{1,0:T(8,128)(2,1)} %w_qkv.1, ...), custom_call_target="tpu_custom_call" | custom-call | tf_op jit(solution)/shard_map/layer/pallas_call | solution.py:509
  108.7 4.0 %hand_over.1 = (bf16[256,1024]{1,0:T(8,128)(2,1)}, f32[128,2048]{1,0:T(8,128)}, f32[2048,128]{1,0:T(8,128)}) custom-call(bf16[256,1024]{1,0:T(8,128)(2,1)} %get-tuple-element.9.layer, f32[128,2048]{1,0:T(8,128)} %get-tuple-element.10.up, f32[2048,128]{1,0:T(8,128)} %get-tuple-element.11.down), custom_call_target="tpu_custom_call" | custom-call | tf_op jit(solution)/shard_map/hand_over/pallas_call | solution.py:528

commit v2 on v1

--- a/solution.py
+++ b/solution.py
@@ -69,6 +69,7 @@
     stage, crecv, r2, rf,
     load_sem, halo_ss, halo_rs, l_ss, l_rs, m_ss, m_rs, x_ss, x_rs, t_ss, t_rs,
     c_ss, c_rs, x2_ss, x2_rs,
+    layer_v, up_v, down_v, layer_sem, up_sem, down_sem,
 ):
     me = lax.axis_index("tile")
     rep = lax.axis_index("rep")
@@ -172,8 +173,9 @@
     def start_sens(which):
         for i in which:
             exchange(i, sens_send, sens_recv, l_ss, l_rs).start()
-            exchange(i, meta_send, meta_recv, m_ss, m_rs).start()
-
+
+    for i in others:
+        exchange(i, meta_send, meta_recv, m_ss, m_rs).start()
     start_sens(range(EARLY))
     sens_recv[me] = sens_send[me]
     meta_recv[me] = meta_send[me]
@@ -263,7 +265,6 @@
     dispatch(moe, 0)
     for i in others:
         exchange(i, feat_send, feat_recv, x_ss, x_rs).start()
-    start_sens(range(EARLY, NE - 1))
     feat_recv[me] = feat_send[me]
 
     disp_t[...] = disp[0:ROWS, :].T
@@ -286,6 +287,9 @@
     own_part = iota((256, ROWS), 0) == lax.div(iota((256, ROWS), 1), CAP) * 16
     other = jnp.sum(jnp.where(own_part, ids, 0.0), axis=0, keepdims=True) - me.astype(f32)
 
+    for i in others:
+        exchange(i, feat_send, feat_recv, x_ss, x_rs).wait_send()
+    start_sens(range(EARLY, NE - 1))
     for i in others:
         arrival(i, feat_send, feat_recv, x_ss, x_rs).wait_recv()
 
@@ -396,57 +400,66 @@
     def finish(g):
         for which in (1, 2, 4, 5):
             hop(g, which).wait_recv()
-        hb = lax.rem(g, NB)
+        parts = []
         for h in range(2):
-            total = (
+            parts.append(
                 stage[g, core, xpos, h].astype(f32)
                 + rf[g, 0, h].astype(f32)
                 + rf[g, 1, h].astype(f32)
             )
-            start = pl.multiple_of(hb * HB + h * 256, 256)
-
-            @pl.when(g < NB)
+        return parts
+
+    def down_copy(hb):
+        rows = pl.ds(pl.multiple_of(hb * HB, HB), HB)
+        return pltpu.make_async_copy(down_v.at[rows, :], out_down.at[rows, :], down_sem.at[hb])
+
+    def up_copy(hb):
+        cols = pl.ds(pl.multiple_of(hb * HB, HB), HB)
+        return pltpu.make_async_copy(up_v.at[:, cols], out_up.at[:, cols], up_sem.at[hb])
+
+    def finish_down(hb, _):
+        for h, total in enumerate(finish(hb)):
+            down_v[pl.ds(pl.multiple_of(hb * HB + h * 256, 256), 256), :] = total
+        down_copy(hb).start()
+        return _
+
+    def finish_up(hb, _):
+        for h, total in enumerate(finish(NB + hb)):
+            up_v[:, pl.ds(pl.multiple_of(hb * HB + h * 256, 256), 256)] = total.T
+        up_copy(hb).start()
+        return _
+
+    def run_groups(first):
+        def body(i, carry):
+            make_pieces(first + i)
+
+            @pl.when(i >= 1)
             def _():
-                out_down[pl.ds(start, 256), :] = total
-
-            @pl.when(g >= NB)
-            def _():
-                out_up[:, pl.ds(start, 256)] = total.T
-
-    def step(s, carry):
-        @pl.when(s < GROUPS)
-        def _():
-            make_pieces(s)
-
-        @pl.when((s >= 1) & (s < GROUPS + 1))
-        def _():
-            add_cores(s - 1)
-
-        @pl.when((s >= 2) & (s < GROUPS + 2))
-        def _():
-            add_far(s - 2)
-
-        @pl.when(s >= 3)
-        def _():
-            finish(s - 3)
-
-        @pl.when(s == 2)
-        def _():
-            drain_sens()
-            make_results(0)
-
-        @pl.when(s == 3)
-        def _():
-            first_grads()
-
-        @pl.when(s == 4)
-        def _():
-            make_results(1)
-            send_results()
-
-        return carry
-
-    lax.fori_loop(0, GROUPS + 3, step, 0)
+                add_cores(first + i - 1)
+
+            return carry
+
+        lax.fori_loop(0, NB, body, 0)
+        add_cores(first + NB - 1)
+
+    run_groups(0)
+    add_far(0)
+    drain_sens()
+    make_results(0)
+    add_far(1)
+    make_results(1)
+    send_results()
+    add_far(2)
+    first_grads()
+    add_far(3)
+    run_groups(NB)
+
+    def far_up(i, _):
+        add_far(NB + i)
+        finish_down(i, 0)
+        return _
+
+    lax.fori_loop(0, NB, far_up, 0)
 
     for i in others:
         arrival(i, rv_send, ret, t_ss, t_rs).wait_recv()
@@ -454,17 +467,23 @@
     def combine(i, _):
         cols = pl.ds(pl.multiple_of(i * 256, 256), 256)
         mixture = dot(disp_t[...], ret[:, :, cols].reshape(ROWS, 256))
-        out_layer[:, cols] = (hid[:, cols] + mixture).astype(bf16)
+        layer_v[:, cols] = (hid[:, cols] + mixture).astype(bf16)
         return _
 
     lax.fori_loop(0, 4, combine, 0)
-
+    layer_copy = pltpu.make_async_copy(layer_v, out_layer, layer_sem)
+    layer_copy.start()
+    lax.fori_loop(0, NB, finish_up, 0)
+
+    layer_copy.wait()
+    for hb in range(NB):
+        down_copy(hb).wait()
+        up_copy(hb).wait()
     for c in halo_copies:
         c.wait_send()
 
     for i in others:
         exchange(i, meta_send, meta_recv, m_ss, m_rs).wait_send()
-        exchange(i, feat_send, feat_recv, x_ss, x_rs).wait_send()
         exchange(i, rv_send, ret, t_ss, t_rs).wait_send()
 
     def drain_groups(g, _):
@@ -476,10 +495,13 @@
     lax.fori_loop(0, GROUPS, drain_groups, 0)
 
 
-def hand_over(layer, up, down, out_layer, out_up, out_down):
-    out_layer[...] = layer[...]
-    out_up[...] = up[...]
-    out_down[...] = down[...]
+def hand_over(layer, up, down, out_layer, out_up, out_down, sem):
+    pairs = ((layer, out_layer), (up, out_up), (down, out_down))
+    copies = [pltpu.make_async_copy(a, b, sem.at[i]) for i, (a, b) in enumerate(pairs)]
+    for c in copies:
+        c.start()
+    for c in copies:
+        c.wait()
 
 
 def on_device(
@@ -505,6 +527,8 @@
         dma((8,)), dma((2,)), dma((2,)),
         dma((NE,)), dma((NE,)), dma((NE,)), dma((NE,)), dma((NE,)), dma((NE,)), dma((NE,)), dma((NE,)),
         dma((GROUPS,)), dma((GROUPS,)), dma((GROUPS, 6)), dma((GROUPS, 6)),
+        buf(T, F), buf(F // 8, FFW, dtype=f32), buf(FFW, F // 8, dtype=f32),
+        dma, dma((NB,)), dma((NB,)),
     ]
     layer, up, down = pl.pallas_call(
         kernel,
@@ -514,7 +538,7 @@
             jax.ShapeDtypeStruct((FFW, F // 8), f32),
         ),
         in_specs=[hbm, vmem, vmem, hbm, hbm, hbm, vmem, hbm, hbm],
-        out_specs=(vmem, vmem, vmem),
+        out_specs=(hbm, hbm, hbm),
         scratch_shapes=scratch,
         compiler_params=pltpu.CompilerParams(
             collective_id=0, has_side_effects=True, vmem_limit_bytes=62 * 1024 * 1024
@@ -524,7 +548,6 @@
         patch_features[0], labels.T, assigned_specialists[0].T, loss_sensitivity[0],
         attn_qkv, attn_out, router.T, expert_up[0], expert_down[0],
     )
-    blocks = [pl.BlockSpec(shape, lambda i: (i, 0)) for shape in ((64, F), (32, FFW), (512, 128))]
     layer, up, down = pl.pallas_call(
         hand_over,
         out_shape=(
@@ -532,9 +555,9 @@
             jax.ShapeDtypeStruct((F // 8, FFW), f32),
             jax.ShapeDtypeStruct((FFW, F // 8), f32),
         ),
-        grid=(4,),
-        in_specs=blocks,
-        out_specs=tuple(blocks),
+        in_specs=[vmem, vmem, vmem],
+        out_specs=(hbm, hbm, hbm),
+        scratch_shapes=[dma((3,))],
         name="hand_over",
     )(layer, up, down)
     return layer[None], up[None], down[None]

time: 114 us -> 104 us (0.912)
  Pallas kernels: 112 us -> 103 us
    pallas_call x1, Pallas kernels: 108 us -> 99.6 us  [on_device(): pl.pallas_call(kernel, out_shape=(jax.ShapeDtypeStruct((T, F), bf16), jax...]
where the time goes in v2:
time: 104 us
  Pallas kernels  103 us (99%)
    pallas_call x1, Pallas kernels, on_device(): pl.pallas_call(kernel, out_shape=(jax.ShapeDtypeStruct((T, F), bf16), jax...  99.6 us
    pallas_call x1, Pallas kernels, on_device(): pl.pallas_call(hand_over, out_shape=(jax.ShapeDtypeStruct((T, F), bf16),...  3.21 us

profile of v2, /device:TPU:1, one launch (start us, length us, event | category | flops | bytes accessed | tf_op | source)
XLA Modules:
  0.0 103.6 jit_solution(10662912442473491602)
XLA Ops:
  0.6 99.6 %layer.1 = (bf16[256,1024]{1,0:T(8,128)(2,1)}, f32[128,2048]{1,0:T(8,128)}, f32[2048,128]{1,0:T(8,128)}) custom-call(bf16[256,1024]{1,0:T(8,128)(2,1)} %bitcast.14, s32[32,128]{1,0:T(8,128)} %bitcast.17, s32[2,256]{1,0:T(2,128)} %bitcast.18, bf16[256,1024]{1,0:T(8,128)(2,1)} %bitcast.15, bf16[1024,3072]{1,0:T(8,128)(2,1)} %w_qkv.1, ...), custom_call_target="tpu_custom_call" | custom-call | tf_op jit(solution)/shard_map/layer/pallas_call | solution.py:533
  100.2 3.2 %hand_over.1 = (bf16[256,1024]{1,0:T(8,128)(2,1)}, f32[128,2048]{1,0:T(8,128)}, f32[2048,128]{1,0:T(8,128)}) custom-call(bf16[256,1024]{1,0:T(8,128)(2,1)} %get-tuple-element.9.layer, f32[128,2048]{1,0:T(8,128)} %get-tuple-element.10.up, f32[2048,128]{1,0:T(8,128)} %get-tuple-element.11.down), custom_call_target="tpu_custom_call" | custom-call | tf_op jit(solution)/shard_map/hand_over/pallas_call | solution.py:551

commit v3 on v2

--- a/solution.py
+++ b/solution.py
@@ -16,7 +16,6 @@
 HB = 512
 NB = FFW // HB
 GROUPS = 2 * NB
-EARLY = 6
 OFFSETS = sorted(
     [(a, b) for a in range(4) for b in range(4) if (a, b) != (0, 0)],
     key=lambda o: -(min(o[0], 4 - o[0]) + min(o[1], 4 - o[1])),
@@ -63,14 +62,15 @@
 def kernel(
     feat, labels, assigned, sens, w_qkv, w_out, router, w_up, w_down,
     out_layer, out_up, out_down,
-    feat_v, sens_v, wq, wk, wv, wo, wu, wd,
+    feat_v, sens_v, w3, wo, wu, wd,
     halo, n_own, n_halo, q_own, k_all, v_all, ctx, oh, hid, moe,
-    disp, disp_t, meta_send, meta_recv, xl_send, xl_recv, ret, a2, gate_v,
+    disp, disp_t, meta_send, meta_recv, x_send, x_recv, l_send, l_recv, l_full, ret, a2, gate_v,
     stage, crecv, r2, rf,
     load_sem, halo_ss, halo_rs, l_ss, l_rs, m_ss, m_rs, x_ss, x_rs, t_ss, t_rs,
     c_ss, c_rs, x2_ss, x2_rs,
     layer_v, up_v, down_v, layer_sem, up_sem, down_sem,
 ):
+    wq, wk, wv = w3.at[0], w3.at[1], w3.at[2]
     me = lax.axis_index("tile")
     rep = lax.axis_index("rep")
     core = lax.rem(rep, 2)
@@ -154,13 +154,16 @@
 
     ld_sens.wait()
 
-    def dispatch(src, kind):
-        for n in range(2):
-            cols = slice(n * 512, n * 512 + 512)
-            block = dot(disp[0:ROWS, :], src[:, cols]).astype(bf16)
-            xl_send[kind, :, :, cols] = block.reshape(NE, CAP, 512)
-
-    dispatch(sens_v, 1)
+    def halves(block):
+        tiles = [block[:, q * 128 : q * 128 + 128] for q in range(8)]
+        return [
+            jnp.concatenate([tiles[q][:, h * 64 : h * 64 + 64] for q in range(8)], axis=1)
+            for h in range(2)
+        ]
+
+    for h, part in enumerate(halves(sens_v[...])):
+        block = dot(disp[0:ROWS, :], part).astype(bf16)
+        l_send[h] = block.reshape(NE, CAP, F // 2)
 
     def make_meta(e, _):
         rows = disp[pl.ds(pl.multiple_of(e * CAP, 16), 128), :]
@@ -168,16 +171,15 @@
         return _
 
     lax.fori_loop(0, NE, make_meta, 0)
-    sens_send, sens_recv = xl_send.at[1], xl_recv.at[1]
-
-    def start_sens(which):
-        for i in which:
-            exchange(i, sens_send, sens_recv, l_ss, l_rs).start()
-
+    def sens_args(h):
+        return l_send.at[h], l_recv.at[h], l_ss.at[h], l_rs.at[h]
+
+    for i in others:
+        exchange(i, *sens_args(0)).start()
     for i in others:
         exchange(i, meta_send, meta_recv, m_ss, m_rs).start()
-    start_sens(range(EARLY))
-    sens_recv[me] = sens_send[me]
+    l_recv[0, me] = l_send[0, me]
+    l_recv[1, me] = l_send[1, me]
     meta_recv[me] = meta_send[me]
 
     ld_feat.wait()
@@ -260,12 +262,13 @@
 
     lax.fori_loop(0, 4, norm_hidden, 0)
 
-    feat_send, feat_recv = xl_send.at[0], xl_recv.at[0]
-
-    dispatch(moe, 0)
-    for i in others:
-        exchange(i, feat_send, feat_recv, x_ss, x_rs).start()
-    feat_recv[me] = feat_send[me]
+    for n in range(2):
+        cols = slice(n * 512, n * 512 + 512)
+        x_send[:, :, cols] = dot(disp[0:ROWS, :], moe[:, cols]).astype(bf16).reshape(NE, CAP, 512)
+    feat_args = (x_send, x_recv, x_ss, x_rs)
+    for i in others:
+        exchange(i, *feat_args).start()
+    x_recv[me] = x_send[me]
 
     disp_t[...] = disp[0:ROWS, :].T
     ld_u.wait()
@@ -277,6 +280,7 @@
         return _
 
     lax.fori_loop(0, 4, transpose_up, 0)
+    ld_d.wait()
 
     for i in others:
         arrival(i, meta_send, meta_recv, m_ss, m_rs).wait_recv()
@@ -288,54 +292,51 @@
     other = jnp.sum(jnp.where(own_part, ids, 0.0), axis=0, keepdims=True) - me.astype(f32)
 
     for i in others:
-        exchange(i, feat_send, feat_recv, x_ss, x_rs).wait_send()
-    start_sens(range(EARLY, NE - 1))
-    for i in others:
-        arrival(i, feat_send, feat_recv, x_ss, x_rs).wait_recv()
-
-    logits = dot(router[...], xl_recv[0].reshape(ROWS, F), NT)
+        exchange(i, *feat_args).wait_send()
+    for i in others:
+        exchange(i, *sens_args(1)).start()
+    for i in others:
+        arrival(i, *feat_args).wait_recv()
+    for i in others:
+        arrival(i, *sens_args(0)).wait_recv()
+
+    logits = dot(router[...], x_recv[...].reshape(ROWS, F), NT)
     sig = 1.0 / (1.0 + jnp.exp(-logits))
     expert = iota((NE, ROWS), 0)
     mine = jnp.sum(jnp.where(expert == me, sig, 0.0), axis=0, keepdims=True)
     theirs = jnp.sum(jnp.where(expert.astype(f32) == other, sig, 0.0), axis=0, keepdims=True)
     gate_v[...] = jnp.broadcast_to(mine / (mine + theirs), (8, ROWS))
 
-    def activate(weight_t, half):
-        def body(i, _):
-            start = pl.multiple_of(i * HB, HB)
-            u = dot(weight_t[pl.ds(start, HB), :], xl_recv[0].reshape(ROWS, F), NT)
-            gate = gate_v[0:1, :]
-            u2 = u * u
-            t = jnp.tanh(GELU_A * u * (1.0 + GELU_B * u2))
-            rise = 0.5 * (1.0 + t)
-            rows = pl.ds(pl.multiple_of(half * F + i * HB, HB), HB)
-            a2[0, rows, :] = (u * rise * gate).astype(bf16)
-            slope = rise + 0.5 * u * (1.0 - t * t) * (GELU_A + (3.0 * GELU_A * GELU_B) * u2)
-            a2[1, rows, :] = (slope * gate).astype(bf16)
-            return _
-
-        lax.fori_loop(0, F // HB, body, 0)
-
-    activate(wk, 0)
-    activate(wv, 1)
-    ld_d.wait()
-    for i in others:
-        arrival(i, sens_send, sens_recv, l_ss, l_rs).wait_recv()
+    def activate(hb):
+        first = pl.multiple_of(lax.rem(hb, 2) * HB, HB)
+        u = dot(w3[1 + lax.div(hb, 2), pl.ds(first, HB), :], x_recv[...].reshape(ROWS, F), NT)
+        gate = gate_v[0:1, :]
+        u2 = u * u
+        t = jnp.tanh(GELU_A * u * (1.0 + GELU_B * u2))
+        rise = 0.5 * (1.0 + t)
+        rows = pl.ds(pl.multiple_of(hb * HB, HB), HB)
+        a2[0, rows, :] = (u * rise * gate).astype(bf16)
+        slope = rise + 0.5 * u * (1.0 - t * t) * (GELU_A + (3.0 * GELU_A * GELU_B) * u2)
+        a2[1, rows, :] = (slope * gate).astype(bf16)
 
     def first_grads():
+        for q in range(4):
+            cols = slice(q * 128, q * 128 + 128)
+            low = l_recv[0, :, :, cols].reshape(ROWS, 128)
+            high = l_recv[1, :, :, cols].reshape(ROWS, 128)
+            l_full[:, q * 256 : q * 256 + 128] = jnp.concatenate([low[:, 0:64], high[:, 0:64]], axis=1)
+            l_full[:, q * 256 + 128 : q * 256 + 256] = jnp.concatenate([low[:, 64:], high[:, 64:]], axis=1)
+
         def body(i, _):
             rows = pl.ds(pl.multiple_of(i * HB, HB), HB)
-            block = dot(wd[rows, :], xl_recv[1].reshape(ROWS, F), NT)
+            block = dot(wd[rows, :], l_full[...], NT)
             a2[1, rows, :] = (block * a2[1, rows, :].astype(f32)).astype(bf16)
             return _
 
         lax.fori_loop(0, NB, body, 0)
 
-    rv_send = sens_send
-
-    def drain_sens():
-        for i in others:
-            exchange(i, sens_send, sens_recv, l_ss, l_rs).wait_send()
+    rv_send = x_send
+    result_args = (rv_send, ret, t_ss, t_rs)
 
     def make_results(half):
         lanes = slice(half * 384, (half + 1) * 384)
@@ -343,32 +344,46 @@
         def product(i, _):
             cols = pl.ds(pl.multiple_of(i * 512, 512), 512)
             block = dot(a2[0, :, lanes], wd[:, cols], TN).astype(bf16)
-            xl_send[1, half * 8 : half * 8 + 8, :, cols] = block.reshape(8, CAP, 512)
+            rv_send[half * 8 : half * 8 + 8, :, cols] = block.reshape(8, CAP, 512)
             return _
 
         lax.fori_loop(0, 2, product, 0)
-
-    def send_results():
         for i in others:
-            exchange(i, rv_send, ret, t_ss, t_rs).start()
-        ret[me] = rv_send[me]
+
+            @pl.when((to_tile[i] >= 8 * half) & (to_tile[i] < 8 * half + 8))
+            def _(i=i):
+                exchange(i, *result_args).start()
 
     def chunk(away):
         return lax.rem(xpos + away, 4)
 
-    def core_copy(g):
-        return rep_copy(stage.at[g, 1 - core], crecv.at[g], c_ss.at[g], c_rs.at[g], partner)
-
-    def make_pieces(g):
-        kind = lax.div(g, NB)
-        rows = pl.ds(pl.multiple_of(lax.rem(g, NB) * HB, HB), HB)
-        block = dot(a2[kind, rows, :], xl_recv[1 - kind].reshape(ROWS, F)).astype(bf16)
+    def core_copy(g, h):
+        return rep_copy(stage.at[g, 1 - core, h], crecv.at[g, h], c_ss.at[g, h], c_rs.at[g, h], partner)
+
+    def down_group(half, hb):
+        return half * 2 + lax.div(hb, 2), lax.rem(hb, 2)
+
+    def make_down(half, hb):
+        g, h = down_group(half, hb)
+        rows = pl.ds(pl.multiple_of(hb * HB, HB), HB)
+        block = dot(a2[0, rows, :], l_recv[half].reshape(ROWS, F // 2)).astype(bf16)
         for q in range(4):
-            for c in range(2):
-                for h in range(2):
+            top = block[0:256, q * 128 : q * 128 + 128]
+            low = block[256:512, q * 128 : q * 128 + 128]
+            stage[g, 0, h, q] = jnp.concatenate([top[:, 0:64], low[:, 0:64]], axis=1)
+            stage[g, 1, h, q] = jnp.concatenate([top[:, 64:], low[:, 64:]], axis=1)
+        core_copy(g, h).start()
+
+    def make_up(hb):
+        g = NB + hb
+        rows = pl.ds(pl.multiple_of(hb * HB, HB), HB)
+        block = dot(a2[1, rows, :], x_recv[...].reshape(ROWS, F)).astype(bf16)
+        for h in range(2):
+            for q in range(4):
+                for c in range(2):
                     start = (2 * q + c) * 128
-                    stage[g, c, q, h] = block[h * 256 : h * 256 + 256, start : start + 128]
-        core_copy(g).start()
+                    stage[g, c, h, q] = block[h * 256 : h * 256 + 256, start : start + 128]
+            core_copy(g, h).start()
 
     def hop(g, which):
         away, h = [(2, 0), (1, 1), (1, 0), (2, 1), (3, 0), (3, 1)][which]
@@ -376,25 +391,41 @@
             r2.at[g, 0], rf.at[g, 0, 1], rf.at[g, 0, 0],
             r2.at[g, 1], rf.at[g, 1, 0], rf.at[g, 1, 1],
         ][which]
-        src = stage.at[g, core, chunk(away), h]
+        src = stage.at[g, core, h, chunk(away)]
         return rep_copy(src, dst, x2_ss.at[g, which], x2_rs.at[g, which], x_next if which < 3 else x_prev)
 
-    def add_cores(g):
-        core_copy(g).wait_recv()
-        for away, sends in ((2, (0, 3)), (1, (1,)), (3, (4,)), (0, ())):
-            q = chunk(away)
-            for h in range(2):
-                total = stage[g, core, q, h].astype(f32) + crecv[g, q, h].astype(f32)
-                stage[g, core, q, h] = total.astype(bf16)
-            for which in sends:
-                hop(g, which).start()
+    def add_cores(g, h):
+        core_copy(g, h).wait_recv()
+        total = stage[g, core, h].astype(f32) + crecv[g, h].astype(f32)
+        stage[g, core, h] = total.astype(bf16)
+
+    def send_half(g, h):
+        for which in ((0, 4), (3, 1))[h]:
+            hop(g, which).start()
+
+    def add_down(half, hb):
+        g, h = down_group(half, hb)
+        add_cores(g, h)
+
+        @pl.when(h == 0)
+        def _():
+            send_half(g, 0)
+
+        @pl.when(h == 1)
+        def _():
+            send_half(g, 1)
+
+    def add_up(hb):
+        for h in range(2):
+            add_cores(NB + hb, h)
+            send_half(NB + hb, h)
 
     def add_far(g):
         for first, away, h, second in ((0, 1, 0, 2), (3, 3, 1, 5)):
             hop(g, first).wait_recv()
             q = chunk(away)
-            total = stage[g, core, q, h].astype(f32) + r2[g, h].astype(f32)
-            stage[g, core, q, h] = total.astype(bf16)
+            total = stage[g, core, h, q].astype(f32) + r2[g, h].astype(f32)
+            stage[g, core, h, q] = total.astype(bf16)
             hop(g, second).start()
 
     def finish(g):
@@ -403,7 +434,7 @@
         parts = []
         for h in range(2):
             parts.append(
-                stage[g, core, xpos, h].astype(f32)
+                stage[g, core, h, xpos].astype(f32)
                 + rf[g, 0, h].astype(f32)
                 + rf[g, 1, h].astype(f32)
             )
@@ -417,10 +448,13 @@
         cols = pl.ds(pl.multiple_of(hb * HB, HB), HB)
         return pltpu.make_async_copy(up_v.at[:, cols], out_up.at[:, cols], up_sem.at[hb])
 
-    def finish_down(hb, _):
-        for h, total in enumerate(finish(hb)):
-            down_v[pl.ds(pl.multiple_of(hb * HB + h * 256, 256), 256), :] = total
-        down_copy(hb).start()
+    def finish_down(pair, _):
+        low, high = finish(pair), finish(2 + pair)
+        for h in range(2):
+            rows = pl.multiple_of((pair * 2 + h) * HB, HB)
+            down_v[pl.ds(rows, 256), :] = jnp.concatenate([low[h][:, 0:64], high[h][:, 0:64]], axis=1)
+            down_v[pl.ds(rows + 256, 256), :] = jnp.concatenate([low[h][:, 64:], high[h][:, 64:]], axis=1)
+            down_copy(pair * 2 + h).start()
         return _
 
     def finish_up(hb, _):
@@ -429,40 +463,67 @@
         up_copy(hb).start()
         return _
 
-    def run_groups(first):
-        def body(i, carry):
-            make_pieces(first + i)
-
-            @pl.when(i >= 1)
+    def down_groups(half, before):
+        def body(hb, carry):
+            before(hb)
+            make_down(half, hb)
+
+            @pl.when(hb >= 1)
             def _():
-                add_cores(first + i - 1)
+                add_down(half, hb - 1)
 
             return carry
 
         lax.fori_loop(0, NB, body, 0)
-        add_cores(first + NB - 1)
-
-    run_groups(0)
+        add_down(half, NB - 1)
+
+    down_groups(0, activate)
     add_far(0)
-    drain_sens()
-    make_results(0)
+    for i in others:
+        arrival(i, *sens_args(1)).wait_recv()
+    down_groups(1, lambda hb: None)
     add_far(1)
-    make_results(1)
-    send_results()
+    first_grads()
     add_far(2)
-    first_grads()
-    add_far(3)
-    run_groups(NB)
-
-    def far_up(i, _):
+
+    def up_step(hb, carry):
+        make_up(hb)
+
+        @pl.when(hb >= 1)
+        def _():
+            add_up(hb - 1)
+
+        @pl.when(hb == 1)
+        def _():
+            make_results(0)
+
+        @pl.when(hb == 2)
+        def _():
+            make_results(1)
+
+        @pl.when(hb >= 2)
+        def _():
+            add_far(hb + 1)
+
+        return carry
+
+    lax.fori_loop(0, NB, up_step, 0)
+    add_up(NB - 1)
+    ret[me] = rv_send[me]
+
+    def far_up(i, carry):
         add_far(NB + i)
-        finish_down(i, 0)
-        return _
-
-    lax.fori_loop(0, NB, far_up, 0)
-
-    for i in others:
-        arrival(i, rv_send, ret, t_ss, t_rs).wait_recv()
+
+        @pl.when(i < 3)
+        def _():
+            finish_down(i - 1, 0)
+
+        return carry
+
+    lax.fori_loop(1, NB, far_up, 0)
+
+    for i in others:
+        arrival(i, *result_args).wait_recv()
 
     def combine(i, _):
         cols = pl.ds(pl.multiple_of(i * 256, 256), 256)
@@ -484,10 +545,13 @@
 
     for i in others:
         exchange(i, meta_send, meta_recv, m_ss, m_rs).wait_send()
-        exchange(i, rv_send, ret, t_ss, t_rs).wait_send()
+        exchange(i, *result_args).wait_send()
+        exchange(i, *sens_args(0)).wait_send()
+        exchange(i, *sens_args(1)).wait_send()
 
     def drain_groups(g, _):
-        core_copy(g).wait_send()
+        for h in range(2):
+            core_copy(g, h).wait_send()
         for which in range(6):
             hop(g, which).wait_send()
         return _
@@ -495,13 +559,24 @@
     lax.fori_loop(0, GROUPS, drain_groups, 0)
 
 
-def hand_over(layer, up, down, out_layer, out_up, out_down, sem):
-    pairs = ((layer, out_layer), (up, out_up), (down, out_down))
-    copies = [pltpu.make_async_copy(a, b, sem.at[i]) for i, (a, b) in enumerate(pairs)]
-    for c in copies:
-        c.start()
-    for c in copies:
-        c.wait()
+def hand_over(layer, up, down, out_layer, out_up, out_down, layer_v, up_v, down_v, sem_in, sem_out):
+    steps = []
+    for a, v, b in ((layer, layer_v, out_layer), (up, up_v, out_up), (down, down_v, out_down)):
+        rows = a.shape[0] // 4
+        for i in range(4):
+            part = pl.ds(i * rows, rows)
+            n = len(steps)
+            steps.append((
+                pltpu.make_async_copy(a.at[part, :], v.at[part, :], sem_in.at[n]),
+                pltpu.make_async_copy(v.at[part, :], b.at[part, :], sem_out.at[n]),
+            ))
+    for first, _ in steps:
+        first.start()
+    for first, second in steps:
+        first.wait()
+        second.start()
+    for _, second in steps:
+        second.wait()
 
 
 def on_device(
@@ -516,17 +591,18 @@
         return pltpu.VMEM(shape, dtype)
 
     scratch = [
-        buf(T, F), buf(T, F), buf(F, F), buf(F, F), buf(F, F), buf(F, F), buf(F, FFW), buf(FFW, F),
+        buf(T, F), buf(T, F), buf(3, F, F), buf(F, F), buf(F, FFW), buf(FFW, F),
         buf(T, F), buf(T, F), buf(T, F), buf(T, F), buf(8, 64, F), buf(8, 64, F), buf(T, F),
         buf(2 * T, 128), buf(T, F, dtype=f32), buf(T, F),
         buf(ROWS + 128 - CAP, T), buf(T, ROWS), buf(NE, 16, 128), buf(NE, 16, 128),
-        buf(2, NE, CAP, F), buf(2, NE, CAP, F), buf(NE, CAP, F), buf(2, FFW, ROWS),
+        buf(NE, CAP, F), buf(NE, CAP, F), buf(2, NE, CAP, F // 2), buf(2, NE, CAP, F // 2), buf(ROWS, F),
+        buf(NE, CAP, F), buf(2, FFW, ROWS),
         buf(8, ROWS, dtype=f32),
-        buf(GROUPS, 2, 4, 2, 256, 128), buf(GROUPS, 4, 2, 256, 128),
+        buf(GROUPS, 2, 2, 4, 256, 128), buf(GROUPS, 2, 4, 256, 128),
         buf(GROUPS, 2, 256, 128), buf(GROUPS, 2, 2, 256, 128),
         dma((8,)), dma((2,)), dma((2,)),
-        dma((NE,)), dma((NE,)), dma((NE,)), dma((NE,)), dma((NE,)), dma((NE,)), dma((NE,)), dma((NE,)),
-        dma((GROUPS,)), dma((GROUPS,)), dma((GROUPS, 6)), dma((GROUPS, 6)),
+        dma((2, NE)), dma((2, NE)), dma((NE,)), dma((NE,)), dma((NE,)), dma((NE,)), dma((NE,)), dma((NE,)),
+        dma((GROUPS, 2)), dma((GROUPS, 2)), dma((GROUPS, 6)), dma((GROUPS, 6)),
         buf(T, F), buf(F // 8, FFW, dtype=f32), buf(FFW, F // 8, dtype=f32),
         dma, dma((NB,)), dma((NB,)),
     ]
@@ -555,9 +631,11 @@
             jax.ShapeDtypeStruct((F // 8, FFW), f32),
             jax.ShapeDtypeStruct((FFW, F // 8), f32),
         ),
-        in_specs=[vmem, vmem, vmem],
+        in_specs=[hbm, hbm, hbm],
         out_specs=(hbm, hbm, hbm),
-        scratch_shapes=[dma((3,))],
+        scratch_shapes=[
+            buf(T, F), buf(F // 8, FFW, dtype=f32), buf(FFW, F // 8, dtype=f32), dma((12,)), dma((12,)),
+        ],
         name="hand_over",
     )(layer, up, down)
     return layer[None], up[None], down[None]

time: 104 us -> 103 us (level)
  the two profiles are of different devices: /device:TPU:1 before, /device:TPU:96 now
where the time goes in v3:
time: 103 us
  Pallas kernels  102 us (99%)
    pallas_call x1, Pallas kernels, on_device(): pl.pallas_call(kernel, out_shape=(jax.ShapeDtypeStruct((T, F), bf16), jax...  99.3 us
    pallas_call x1, Pallas kernels, on_device(): pl.pallas_call(hand_over, out_shape=(jax.ShapeDtypeStruct((T, F), bf16),...  2.73 us

profile of v3, /device:TPU:96, one launch (start us, length us, event | category | flops | bytes accessed | tf_op | source)
XLA Modules:
  0.0 102.8 jit_solution(7674443167373765483)
XLA Ops:
  0.6 99.3 %layer.1 = (bf16[256,1024]{1,0:T(8,128)(2,1)}, f32[128,2048]{1,0:T(8,128)}, f32[2048,128]{1,0:T(8,128)}) custom-call(bf16[256,1024]{1,0:T(8,128)(2,1)} %bitcast.14, s32[32,128]{1,0:T(8,128)} %bitcast.17, s32[2,256]{1,0:T(2,128)} %bitcast.18, bf16[256,1024]{1,0:T(8,128)(2,1)} %bitcast.15, bf16[1024,3072]{1,0:T(8,128)(2,1)} %w_qkv.1, ...), custom_call_target="tpu_custom_call" | custom-call | tf_op jit(solution)/shard_map/layer/pallas_call | solution.py:609
  99.9 2.7 %hand_over.1 = (bf16[256,1024]{1,0:T(8,128)(2,1)}, f32[128,2048]{1,0:T(8,128)}, f32[2048,128]{1,0:T(8,128)}) custom-call(bf16[256,1024]{1,0:T(8,128)(2,1)} %get-tuple-element.9.layer, f32[128,2048]{1,0:T(8,128)} %get-tuple-element.10.up, f32[2048,128]{1,0:T(8,128)} %get-tuple-element.11.down), custom_call_target="tpu_custom_call" | custom-call | tf_op jit(solution)/shard_map/hand_over/pallas_call | solution.py:627

commit v4 on v3

--- a/solution.py
+++ b/solution.py
@@ -64,7 +64,7 @@
     out_layer, out_up, out_down,
     feat_v, sens_v, w3, wo, wu, wd,
     halo, n_own, n_halo, q_own, k_all, v_all, ctx, oh, hid, moe,
-    disp, disp_t, meta_send, meta_recv, x_send, x_recv, l_send, l_recv, l_full, ret, a2, gate_v,
+    disp, disp_t, meta_send, meta_recv, x_send, x_recv, l_send, l_recv, slope_v, ret, a2, gate_v,
     stage, crecv, r2, rf,
     load_sem, halo_ss, halo_rs, l_ss, l_rs, m_ss, m_rs, x_ss, x_rs, t_ss, t_rs,
     c_ss, c_rs, x2_ss, x2_rs,
@@ -282,6 +282,28 @@
     lax.fori_loop(0, 4, transpose_up, 0)
     ld_d.wait()
 
+    def split_down(i, _):
+        rows = pl.ds(pl.multiple_of(lax.rem(i, 4) * 256, 256), 256)
+        for h, part in enumerate(halves(wd[pl.ds(pl.multiple_of(i * 256, 256), 256), :])):
+            wu[rows, pl.ds(pl.multiple_of(h * F + lax.div(i, 4) * HB, HB), HB)] = part
+        return _
+
+    lax.fori_loop(0, 8, split_down, 0)
+
+    def half_grads(half, hb):
+        rows = pl.ds(pl.multiple_of(lax.rem(hb, 2) * HB, HB), HB)
+        cols = pl.ds(pl.multiple_of(half * F + lax.div(hb, 2) * HB, HB), HB)
+        return dot(wu[rows, cols], l_recv[half].reshape(ROWS, F // 2), NT)
+
+    for i in others:
+        arrival(i, *sens_args(0)).wait_recv()
+
+    def first_half(hb, _):
+        a2[1, pl.ds(pl.multiple_of(hb * HB, HB), HB), :] = half_grads(0, hb).astype(bf16)
+        return _
+
+    lax.fori_loop(0, NB, first_half, 0)
+
     for i in others:
         arrival(i, meta_send, meta_recv, m_ss, m_rs).wait_recv()
 
@@ -297,8 +319,6 @@
         exchange(i, *sens_args(1)).start()
     for i in others:
         arrival(i, *feat_args).wait_recv()
-    for i in others:
-        arrival(i, *sens_args(0)).wait_recv()
 
     logits = dot(router[...], x_recv[...].reshape(ROWS, F), NT)
     sig = 1.0 / (1.0 + jnp.exp(-logits))
@@ -317,23 +337,13 @@
         rows = pl.ds(pl.multiple_of(hb * HB, HB), HB)
         a2[0, rows, :] = (u * rise * gate).astype(bf16)
         slope = rise + 0.5 * u * (1.0 - t * t) * (GELU_A + (3.0 * GELU_A * GELU_B) * u2)
-        a2[1, rows, :] = (slope * gate).astype(bf16)
-
-    def first_grads():
-        for q in range(4):
-            cols = slice(q * 128, q * 128 + 128)
-            low = l_recv[0, :, :, cols].reshape(ROWS, 128)
-            high = l_recv[1, :, :, cols].reshape(ROWS, 128)
-            l_full[:, q * 256 : q * 256 + 128] = jnp.concatenate([low[:, 0:64], high[:, 0:64]], axis=1)
-            l_full[:, q * 256 + 128 : q * 256 + 256] = jnp.concatenate([low[:, 64:], high[:, 64:]], axis=1)
-
-        def body(i, _):
-            rows = pl.ds(pl.multiple_of(i * HB, HB), HB)
-            block = dot(wd[rows, :], l_full[...], NT)
-            a2[1, rows, :] = (block * a2[1, rows, :].astype(f32)).astype(bf16)
-            return _
-
-        lax.fori_loop(0, NB, body, 0)
+        slope_v[rows, :] = (slope * gate).astype(bf16)
+
+    def first_grads(hb, _):
+        rows = pl.ds(pl.multiple_of(hb * HB, HB), HB)
+        block = half_grads(1, hb) + a2[1, rows, :].astype(f32)
+        a2[1, rows, :] = (block * slope_v[rows, :].astype(f32)).astype(bf16)
+        return _
 
     rv_send = x_send
     result_args = (rv_send, ret, t_ss, t_rs)
@@ -419,6 +429,11 @@
         for h in range(2):
             add_cores(NB + hb, h)
             send_half(NB + hb, h)
+
+    def add_last():
+        for h, which in ((0, 0), (1, 3)):
+            add_cores(GROUPS - 1, h)
+            hop(GROUPS - 1, which).start()
 
     def add_far(g):
         for first, away, h, second in ((0, 1, 0, 2), (3, 3, 1, 5)):
@@ -483,8 +498,12 @@
         arrival(i, *sens_args(1)).wait_recv()
     down_groups(1, lambda hb: None)
     add_far(1)
-    first_grads()
+    make_results(0)
     add_far(2)
+    make_results(1)
+    ret[me] = rv_send[me]
+    add_far(3)
+    lax.fori_loop(0, NB, first_grads, 0)
 
     def up_step(hb, carry):
         make_up(hb)
@@ -493,34 +512,20 @@
         def _():
             add_up(hb - 1)
 
-        @pl.when(hb == 1)
-        def _():
-            make_results(0)
-
-        @pl.when(hb == 2)
-        def _():
-            make_results(1)
-
         @pl.when(hb >= 2)
         def _():
-            add_far(hb + 1)
+            add_far(NB + hb - 2)
 
         return carry
 
     lax.fori_loop(0, NB, up_step, 0)
-    add_up(NB - 1)
-    ret[me] = rv_send[me]
-
-    def far_up(i, carry):
-        add_far(NB + i)
-
-        @pl.when(i < 3)
-        def _():
-            finish_down(i - 1, 0)
-
-        return carry
-
-    lax.fori_loop(1, NB, far_up, 0)
+    add_last()
+    add_far(GROUPS - 2)
+    finish_down(0, 0)
+    add_far(GROUPS - 1)
+    for which in (1, 4):
+        hop(GROUPS - 1, which).start()
+    finish_down(1, 0)
 
     for i in others:
         arrival(i, *result_args).wait_recv()
@@ -595,7 +600,7 @@
         buf(T, F), buf(T, F), buf(T, F), buf(T, F), buf(8, 64, F), buf(8, 64, F), buf(T, F),
         buf(2 * T, 128), buf(T, F, dtype=f32), buf(T, F),
         buf(ROWS + 128 - CAP, T), buf(T, ROWS), buf(NE, 16, 128), buf(NE, 16, 128),
-        buf(NE, CAP, F), buf(NE, CAP, F), buf(2, NE, CAP, F // 2), buf(2, NE, CAP, F // 2), buf(ROWS, F),
+        buf(NE, CAP, F), buf(NE, CAP, F), buf(2, NE, CAP, F // 2), buf(2, NE, CAP, F // 2), buf(FFW, ROWS),
         buf(NE, CAP, F), buf(2, FFW, ROWS),
         buf(8, ROWS, dtype=f32),
         buf(GROUPS, 2, 2, 4, 256, 128), buf(GROUPS, 2, 4, 256, 128),

time: 103 us -> 101 us (0.981)
  the two profiles are of different devices: /device:TPU:96 before, /device:TPU:1 now
where the time goes in v4:
time: 101 us; the launch traced here: 98.8 us
  Pallas kernels  98 us (97%)
    pallas_call x1, Pallas kernels, on_device(): pl.pallas_call(kernel, out_shape=(jax.ShapeDtypeStruct((T, F), bf16), jax...  95.3 us
    pallas_call x1, Pallas kernels, on_device(): pl.pallas_call(hand_over, out_shape=(jax.ShapeDtypeStruct((T, F), bf16),...  2.73 us

profile of v4, /device:TPU:1, one launch (start us, length us, event | category | flops | bytes accessed | tf_op | source)
XLA Modules:
  0.0 98.8 jit_solution(5255716832119731075)
XLA Ops:
  0.6 95.3 %layer.1 = (bf16[256,1024]{1,0:T(8,128)(2,1)}, f32[128,2048]{1,0:T(8,128)}, f32[2048,128]{1,0:T(8,128)}) custom-call(bf16[256,1024]{1,0:T(8,128)(2,1)} %bitcast.14, s32[32,128]{1,0:T(8,128)} %bitcast.17, s32[2,256]{1,0:T(2,128)} %bitcast.18, bf16[256,1024]{1,0:T(8,128)(2,1)} %bitcast.15, bf16[1024,3072]{1,0:T(8,128)(2,1)} %w_qkv.1, ...), custom_call_target="tpu_custom_call" | custom-call | tf_op jit(solution)/shard_map/layer/pallas_call | solution.py:614
  95.9 2.7 %hand_over.1 = (bf16[256,1024]{1,0:T(8,128)(2,1)}, f32[128,2048]{1,0:T(8,128)}, f32[2048,128]{1,0:T(8,128)}) custom-call(bf16[256,1024]{1,0:T(8,128)(2,1)} %get-tuple-element.9.layer, f32[128,2048]{1,0:T(8,128)} %get-tuple-element.10.up, f32[2048,128]{1,0:T(8,128)} %get-tuple-element.11.down), custom_call_target="tpu_custom_call" | custom-call | tf_op jit(solution)/shard_map/hand_over/pallas_call | solution.py:632

commit v5 on v4

--- a/solution.py
+++ b/solution.py
@@ -174,10 +174,9 @@
     def sens_args(h):
         return l_send.at[h], l_recv.at[h], l_ss.at[h], l_rs.at[h]
 
-    for i in others:
+    along_z = [i for i in others if OFFSETS[i][0] == 0]
+    for i in along_z:
         exchange(i, *sens_args(0)).start()
-    for i in others:
-        exchange(i, meta_send, meta_recv, m_ss, m_rs).start()
     l_recv[0, me] = l_send[0, me]
     l_recv[1, me] = l_send[1, me]
     meta_recv[me] = meta_send[me]
@@ -213,6 +212,11 @@
 
     for c in halo_copies:
         c.wait_recv()
+    for i in others:
+        if i not in along_z:
+            exchange(i, *sens_args(0)).start()
+    for i in others:
+        exchange(i, meta_send, meta_recv, m_ss, m_rs).start()
     norm_to_windows(halo, n_halo, range(4))
     project(n_halo, wk, k_all, 32)
     project(n_halo, wv, v_all, 32)
@@ -314,11 +318,11 @@
     other = jnp.sum(jnp.where(own_part, ids, 0.0), axis=0, keepdims=True) - me.astype(f32)
 
     for i in others:
+        arrival(i, *feat_args).wait_recv()
+    for i in others:
         exchange(i, *feat_args).wait_send()
     for i in others:
         exchange(i, *sens_args(1)).start()
-    for i in others:
-        arrival(i, *feat_args).wait_recv()
 
     logits = dot(router[...], x_recv[...].reshape(ROWS, F), NT)
     sig = 1.0 / (1.0 + jnp.exp(-logits))
@@ -499,10 +503,8 @@
     down_groups(1, lambda hb: None)
     add_far(1)
     make_results(0)
-    add_far(2)
     make_results(1)
     ret[me] = rv_send[me]
-    add_far(3)
     lax.fori_loop(0, NB, first_grads, 0)
 
     def up_step(hb, carry):
@@ -512,14 +514,15 @@
         def _():
             add_up(hb - 1)
 
-        @pl.when(hb >= 2)
+        @pl.when(hb >= 1)
         def _():
-            add_far(NB + hb - 2)
+            add_far(hb + 1)
 
         return carry
 
     lax.fori_loop(0, NB, up_step, 0)
     add_last()
+    add_far(GROUPS - 3)
     add_far(GROUPS - 2)
     finish_down(0, 0)
     add_far(GROUPS - 1)

time: 101 us -> 101 us (level); the launches traced: 98.8 us -> 101 us
  Pallas kernels: 98 us -> 100 us
    pallas_call x1, Pallas kernels: 95.3 us -> 97.2 us  [on_device(): pl.pallas_call(kernel, out_shape=(jax.ShapeDtypeStruct((T, F), bf16), jax...]
where the time goes in v5:
time: 101 us
  Pallas kernels  100 us (99%)
    pallas_call x1, Pallas kernels, on_device(): pl.pallas_call(kernel, out_shape=(jax.ShapeDtypeStruct((T, F), bf16), jax...  97.2 us
    pallas_call x1, Pallas kernels, on_device(): pl.pallas_call(hand_over, out_shape=(jax.ShapeDtypeStruct((T, F), bf16),...  2.73 us

profile of v5, /device:TPU:1, one launch (start us, length us, event | category | flops | bytes accessed | tf_op | source)
XLA Modules:
  0.0 100.8 jit_solution(3658840531301869331)
XLA Ops:
  0.6 97.2 %layer.1 = (bf16[256,1024]{1,0:T(8,128)(2,1)}, f32[128,2048]{1,0:T(8,128)}, f32[2048,128]{1,0:T(8,128)}) custom-call(bf16[256,1024]{1,0:T(8,128)(2,1)} %bitcast.14, s32[32,128]{1,0:T(8,128)} %bitcast.17, s32[2,256]{1,0:T(2,128)} %bitcast.18, bf16[256,1024]{1,0:T(8,128)(2,1)} %bitcast.15, bf16[1024,3072]{1,0:T(8,128)(2,1)} %w_qkv.1, ...), custom_call_target="tpu_custom_call" | custom-call | tf_op jit(solution)/shard_map/layer/pallas_call | solution.py:617
  97.9 2.7 %hand_over.1 = (bf16[256,1024]{1,0:T(8,128)(2,1)}, f32[128,2048]{1,0:T(8,128)}, f32[2048,128]{1,0:T(8,128)}) custom-call(bf16[256,1024]{1,0:T(8,128)(2,1)} %get-tuple-element.9.layer, f32[128,2048]{1,0:T(8,128)} %get-tuple-element.10.up, f32[2048,128]{1,0:T(8,128)} %get-tuple-element.11.down), custom_call_target="tpu_custom_call" | custom-call | tf_op jit(solution)/shard_map/hand_over/pallas_call | solution.py:635

commit v6 on v5

--- a/solution.py
+++ b/solution.py
@@ -18,7 +18,7 @@
 GROUPS = 2 * NB
 OFFSETS = sorted(
     [(a, b) for a in range(4) for b in range(4) if (a, b) != (0, 0)],
-    key=lambda o: -(min(o[0], 4 - o[0]) + min(o[1], 4 - o[1])),
+    key=lambda o: min(o[0], 4 - o[0]) + min(o[1], 4 - o[1]),
 )
 QW = 256
 SCALE = 32 ** (-0.5)
@@ -130,13 +130,13 @@
         c.start()
 
     def exchange(i, src, dst, ss, rs):
-        t = to_tile[i]
-        return tile_copy(src.at[t], dst.at[me], ss.at[i], rs.at[i], t)
+        return tile_copy(src.at[to_tile[i]], dst.at[i], ss.at[i], rs.at[i], to_tile[i])
 
     def arrival(i, src, dst, ss, rs):
-        t = from_tile[i]
-        return tile_copy(src.at[t], dst.at[t], ss.at[i], rs.at[i], t)
-
+        return tile_copy(src.at[from_tile[i]], dst.at[i], ss.at[i], rs.at[i], from_tile[i])
+
+    last = NE - 1
+    near, far = range(NE // 2), range(NE // 2, NE - 1)
     others = range(NE - 1)
 
     ids_t = assigned[...]
@@ -177,9 +177,9 @@
     along_z = [i for i in others if OFFSETS[i][0] == 0]
     for i in along_z:
         exchange(i, *sens_args(0)).start()
-    l_recv[0, me] = l_send[0, me]
-    l_recv[1, me] = l_send[1, me]
-    meta_recv[me] = meta_send[me]
+    l_recv[0, last] = l_send[0, me]
+    l_recv[1, last] = l_send[1, me]
+    meta_recv[last] = meta_send[me]
 
     ld_feat.wait()
     norm_to_windows(feat_v, n_own, range(4))
@@ -270,9 +270,9 @@
         cols = slice(n * 512, n * 512 + 512)
         x_send[:, :, cols] = dot(disp[0:ROWS, :], moe[:, cols]).astype(bf16).reshape(NE, CAP, 512)
     feat_args = (x_send, x_recv, x_ss, x_rs)
-    for i in others:
+    for i in near:
         exchange(i, *feat_args).start()
-    x_recv[me] = x_send[me]
+    x_recv[last] = x_send[me]
 
     disp_t[...] = disp[0:ROWS, :].T
     ld_u.wait()
@@ -317,31 +317,39 @@
     own_part = iota((256, ROWS), 0) == lax.div(iota((256, ROWS), 1), CAP) * 16
     other = jnp.sum(jnp.where(own_part, ids, 0.0), axis=0, keepdims=True) - me.astype(f32)
 
-    for i in others:
-        arrival(i, *feat_args).wait_recv()
-    for i in others:
+    for i in near:
         exchange(i, *feat_args).wait_send()
-    for i in others:
-        exchange(i, *sens_args(1)).start()
-
-    logits = dot(router[...], x_recv[...].reshape(ROWS, F), NT)
-    sig = 1.0 / (1.0 + jnp.exp(-logits))
-    expert = iota((NE, ROWS), 0)
-    mine = jnp.sum(jnp.where(expert == me, sig, 0.0), axis=0, keepdims=True)
-    theirs = jnp.sum(jnp.where(expert.astype(f32) == other, sig, 0.0), axis=0, keepdims=True)
-    gate_v[...] = jnp.broadcast_to(mine / (mine + theirs), (8, ROWS))
-
-    def activate(hb):
+    for i in far:
+        exchange(i, *feat_args).start()
+
+    def lanes_of(half):
+        return slice(half * 384, half * 384 + 384)
+
+    def half_rows(half):
+        return x_recv[half * 8 : half * 8 + 8].reshape(ROWS // 2, F)
+
+    def make_gates(half):
+        lanes = lanes_of(half)
+        logits = dot(router[...], half_rows(half), NT)
+        sig = 1.0 / (1.0 + jnp.exp(-logits))
+        expert = iota((NE, ROWS // 2), 0)
+        mine = jnp.sum(jnp.where(expert == me, sig, 0.0), axis=0, keepdims=True)
+        theirs = jnp.where(expert.astype(f32) == other[:, lanes], sig, 0.0)
+        theirs = jnp.sum(theirs, axis=0, keepdims=True)
+        gate_v[:, lanes] = jnp.broadcast_to(mine / (mine + theirs), (8, ROWS // 2))
+
+    def activate(hb, half):
+        lanes = lanes_of(half)
         first = pl.multiple_of(lax.rem(hb, 2) * HB, HB)
-        u = dot(w3[1 + lax.div(hb, 2), pl.ds(first, HB), :], x_recv[...].reshape(ROWS, F), NT)
-        gate = gate_v[0:1, :]
+        u = dot(w3[1 + lax.div(hb, 2), pl.ds(first, HB), :], half_rows(half), NT)
+        gate = gate_v[0:1, lanes]
         u2 = u * u
         t = jnp.tanh(GELU_A * u * (1.0 + GELU_B * u2))
         rise = 0.5 * (1.0 + t)
         rows = pl.ds(pl.multiple_of(hb * HB, HB), HB)
-        a2[0, rows, :] = (u * rise * gate).astype(bf16)
+        a2[0, rows, lanes] = (u * rise * gate).astype(bf16)
         slope = rise + 0.5 * u * (1.0 - t * t) * (GELU_A + (3.0 * GELU_A * GELU_B) * u2)
-        slope_v[rows, :] = (slope * gate).astype(bf16)
+        slope_v[rows, lanes] = (slope * gate).astype(bf16)
 
     def first_grads(hb, _):
         rows = pl.ds(pl.multiple_of(hb * HB, HB), HB)
@@ -349,24 +357,38 @@
         a2[1, rows, :] = (block * slope_v[rows, :].astype(f32)).astype(bf16)
         return _
 
-    rv_send = x_send
-    result_args = (rv_send, ret, t_ss, t_rs)
+    def send_result(i):
+        block = w3.at[0, i * CAP : i * CAP + CAP, :]
+        return tile_copy(block, ret.at[me], t_ss.at[i], t_rs.at[i], from_tile[i])
+
+    def result_arrival(i):
+        block = w3.at[0, i * CAP : i * CAP + CAP, :]
+        return tile_copy(block, ret.at[to_tile[i]], t_ss.at[i], t_rs.at[i], from_tile[i])
 
     def make_results(half):
-        lanes = slice(half * 384, (half + 1) * 384)
-
         def product(i, _):
             cols = pl.ds(pl.multiple_of(i * 512, 512), 512)
-            block = dot(a2[0, :, lanes], wd[:, cols], TN).astype(bf16)
-            rv_send[half * 8 : half * 8 + 8, :, cols] = block.reshape(8, CAP, 512)
+            block = dot(a2[0, :, lanes_of(half)], wd[:, cols], TN).astype(bf16)
+            w3[0, half * 384 : half * 384 + 384, cols] = block
             return _
 
         lax.fori_loop(0, 2, product, 0)
-        for i in others:
-
-            @pl.when((to_tile[i] >= 8 * half) & (to_tile[i] < 8 * half + 8))
-            def _(i=i):
-                exchange(i, *result_args).start()
+
+    for i in near:
+        arrival(i, *feat_args).wait_recv()
+    make_gates(0)
+
+    def near_step(hb, carry):
+        activate(hb, 0)
+        return carry
+
+    lax.fori_loop(0, NB, near_step, 0)
+    make_results(0)
+    for i in far:
+        arrival(i, *feat_args).wait_recv()
+    for i in others:
+        exchange(i, *sens_args(1)).start()
+    make_gates(1)
 
     def chunk(away):
         return lax.rem(xpos + away, 4)
@@ -482,29 +504,40 @@
         up_copy(hb).start()
         return _
 
-    def down_groups(half, before):
-        def body(hb, carry):
-            before(hb)
-            make_down(half, hb)
-
-            @pl.when(hb >= 1)
-            def _():
-                add_down(half, hb - 1)
-
-            return carry
-
-        lax.fori_loop(0, NB, body, 0)
-        add_down(half, NB - 1)
-
-    down_groups(0, activate)
+    def first_half_step(hb, carry):
+        activate(hb, 1)
+
+        @pl.when(hb >= 1)
+        def _():
+            add_down(0, hb - 1)
+
+        make_down(0, hb)
+        return carry
+
+    lax.fori_loop(0, NB, first_half_step, 0)
     add_far(0)
+    add_down(0, NB - 1)
     for i in others:
         arrival(i, *sens_args(1)).wait_recv()
-    down_groups(1, lambda hb: None)
+    for i in near:
+        send_result(i).start()
+
+    def second_half_step(hb, carry):
+        make_down(1, hb)
+
+        @pl.when(hb >= 1)
+        def _():
+            add_down(1, hb - 1)
+
+        return carry
+
+    lax.fori_loop(0, NB, second_half_step, 0)
+    add_down(1, NB - 1)
     add_far(1)
-    make_results(0)
     make_results(1)
-    ret[me] = rv_send[me]
+    for i in far:
+        send_result(i).start()
+    ret[me] = w3[0, last * CAP : ROWS, :]
     lax.fori_loop(0, NB, first_grads, 0)
 
     def up_step(hb, carry):
@@ -531,7 +564,7 @@
     finish_down(1, 0)
 
     for i in others:
-        arrival(i, *result_args).wait_recv()
+        result_arrival(i).wait_recv()
 
     def combine(i, _):
         cols = pl.ds(pl.multiple_of(i * 256, 256), 256)
@@ -553,7 +586,9 @@
 
     for i in others:
         exchange(i, meta_send, meta_recv, m_ss, m_rs).wait_send()
-        exchange(i, *result_args).wait_send()
+        if i in far:
+            exchange(i, *feat_args).wait_send()
+        send_result(i).wait_send()
         exchange(i, *sens_args(0)).wait_send()
         exchange(i, *sens_args(1)).wait_send()
 

time: 101 us -> 106 us (1.050); the launches traced: 101 us -> 104 us
  Pallas kernels: 100 us -> 103 us
    pallas_call x1, Pallas kernels: 97.2 us -> 100 us  [on_device(): pl.pallas_call(kernel, out_shape=(jax.ShapeDtypeStruct((T, F), bf16), jax...]
where the time goes in v6:
time: 106 us; the launch traced here: 104 us
  Pallas kernels  103 us (97%)
    pallas_call x1, Pallas kernels, on_device(): pl.pallas_call(kernel, out_shape=(jax.ShapeDtypeStruct((T, F), bf16), jax...  100 us
    pallas_call x1, Pallas kernels, on_device(): pl.pallas_call(hand_over, out_shape=(jax.ShapeDtypeStruct((T, F), bf16),...  2.73 us

profile of v6, /device:TPU:1, one launch (start us, length us, event | category | flops | bytes accessed | tf_op | source)
XLA Modules:
  0.0 104.0 jit_solution(15507779108153923194)
XLA Ops:
  0.6 100.4 %layer.1 = (bf16[256,1024]{1,0:T(8,128)(2,1)}, f32[128,2048]{1,0:T(8,128)}, f32[2048,128]{1,0:T(8,128)}) custom-call(bf16[256,1024]{1,0:T(8,128)(2,1)} %bitcast.14, s32[32,128]{1,0:T(8,128)} %bitcast.17, s32[2,256]{1,0:T(2,128)} %bitcast.18, bf16[256,1024]{1,0:T(8,128)(2,1)} %bitcast.15, bf16[1024,3072]{1,0:T(8,128)(2,1)} %w_qkv.1, ...), custom_call_target="tpu_custom_call" | custom-call | tf_op jit(solution)/shard_map/layer/pallas_call | solution.py:652
  101.1 2.7 %hand_over.1 = (bf16[256,1024]{1,0:T(8,128)(2,1)}, f32[128,2048]{1,0:T(8,128)}, f32[2048,128]{1,0:T(8,128)}) custom-call(bf16[256,1024]{1,0:T(8,128)(2,1)} %get-tuple-element.9.layer, f32[128,2048]{1,0:T(8,128)} %get-tuple-element.10.up, f32[2048,128]{1,0:T(8,128)} %get-tuple-element.11.down), custom_call_target="tpu_custom_call" | custom-call | tf_op jit(solution)/shard_map/hand_over/pallas_call | solution.py:670

commit v7 on v4

--- a/solution.py
+++ b/solution.py
@@ -314,11 +314,11 @@
     other = jnp.sum(jnp.where(own_part, ids, 0.0), axis=0, keepdims=True) - me.astype(f32)
 
     for i in others:
+        arrival(i, *feat_args).wait_recv()
+    for i in others:
         exchange(i, *feat_args).wait_send()
     for i in others:
         exchange(i, *sens_args(1)).start()
-    for i in others:
-        arrival(i, *feat_args).wait_recv()
 
     logits = dot(router[...], x_recv[...].reshape(ROWS, F), NT)
     sig = 1.0 / (1.0 + jnp.exp(-logits))

time: 101 us -> 99.1 us (0.981); the launches traced: 98.8 us -> 98.9 us
  no operation moved by 1% of the time
where the time goes in v7:
time: 99.1 us; the launch traced here: 98.9 us
  Pallas kernels  98.1 us (99%)
    pallas_call x1, Pallas kernels, on_device(): pl.pallas_call(kernel, out_shape=(jax.ShapeDtypeStruct((T, F), bf16), jax...  95.3 us
    pallas_call x1, Pallas kernels, on_device(): pl.pallas_call(hand_over, out_shape=(jax.ShapeDtypeStruct((T, F), bf16),...  2.73 us

profile of v7, /device:TPU:1, one launch (start us, length us, event | category | flops | bytes accessed | tf_op | source)
XLA Modules:
  0.0 98.9 jit_solution(2047950090495405313)
XLA Ops:
  0.6 95.3 %layer.1 = (bf16[256,1024]{1,0:T(8,128)(2,1)}, f32[128,2048]{1,0:T(8,128)}, f32[2048,128]{1,0:T(8,128)}) custom-call(bf16[256,1024]{1,0:T(8,128)(2,1)} %bitcast.14, s32[32,128]{1,0:T(8,128)} %bitcast.17, s32[2,256]{1,0:T(2,128)} %bitcast.18, bf16[256,1024]{1,0:T(8,128)(2,1)} %bitcast.15, bf16[1024,3072]{1,0:T(8,128)(2,1)} %w_qkv.1, ...), custom_call_target="tpu_custom_call" | custom-call | tf_op jit(solution)/shard_map/layer/pallas_call | solution.py:614
  96.0 2.7 %hand_over.1 = (bf16[256,1024]{1,0:T(8,128)(2,1)}, f32[128,2048]{1,0:T(8,128)}, f32[2048,128]{1,0:T(8,128)}) custom-call(bf16[256,1024]{1,0:T(8,128)(2,1)} %get-tuple-element.9.layer, f32[128,2048]{1,0:T(8,128)} %get-tuple-element.10.up, f32[2048,128]{1,0:T(8,128)} %get-tuple-element.11.down), custom_call_target="tpu_custom_call" | custom-call | tf_op jit(solution)/shard_map/hand_over/pallas_call | solution.py:632
